TPU v7x, 128 devices: a whole 4x4x4 slice. The times are simulated.
128 devices in a mesh: group: 4 (over z), dom: 32 (over x, y, core).
Axes of the slice: x: 4, y: 4, z: 4, core: 2. Of those that a mesh axis runs over, the one named last changes fastest.
Arguments:
- positions: float32 [4, 3, 262144], P('group', None, 'dom'), as said below
- velocity: float32 [4, 3, 262144], P('group', None, 'dom'), may hold values from -6 to 6
- mass: float32 [4, 262144], P('group', 'dom'), may hold values from 0.5 to 2
- stress: float32 [4, 3, 262144], P('group', None, 'dom'), may hold values from -6 to 6
- corner_block: int32 [4, 4, 2048], P('group', None, 'dom'), may hold values from 0 to 64, as said below
- corner_slot: int32 [4, 4, 262144], P('group', None, 'dom'), may hold values from 0 to 127, as said below
- halo_block: int32 [4, 32], P('group', 'dom'), may hold values from 0 to 63
- contact_owner: int32 [4, 2048], P('group', 'dom'), may hold values from -1 to 127, as said below
- contact_slot: int32 [4, 2048], P('group', 'dom'), may hold values from -1 to 31, as said below
- tile_pairs: int32 [4, 2, 768], P('group', None, 'dom'), may hold values from 0 to 31, as said below
- tile_active: int32 [4, 768], P('group', 'dom'), may hold values from 0 to 1
Outputs:
- velocity_next: float32 [4, 3, 262144], P('group', None, 'dom')
- stress_next: float32 [4, 3, 262144], P('group', None, 'dom')
Inputs may be any that keep to these rules, and one draw needn't show every extreme that they name: `positions`: every element is a quadrilateral whose normal diag_a x diag_b has length 0.1 or more and whose vector diag_a - diag_b keeps a length of 0.5 or more off that normal. `corner_block`: in every element block corners 0 and 3 name one node block and corners 1 and 2 another; the value 64 names the shared block of the next partition (cyclic), given by halo_block. `corner_slot`: for each corner, the 128 elements of an element block name 128 different slots. `contact_owner`: -1 marks a node block without contact. Otherwise, for a block of the partition with dom index d, the owner's dom index (owner mod 32) is d - 1, d or d + 1, cyclic; at most 8 blocks of one partition go to one owner. `contact_slot`: -1 exactly where contact_owner is -1. Otherwise slot // 8 is the block's layer index, and no two blocks share an owner and a slot. `tile_pairs`: both slots of a tile with flag 1 hold a block at that owner.
All inputs are finite; a program needn't handle non-finite values.
Results may differ from a plain program's by a relative error of at most 0.0003.
Values sent between devices are 32-bit elements; how exact they have to be, the bound alone decides.
A program may use at most 64 MiB of HBM per device.

v0:
```python
import math

import jax
import jax.numpy as jnp
from jax import lax
from jax.sharding import PartitionSpec as P

CYCLE = 128


DT = 0.5
STIFF = 2.0
POISSON = 0.3
HOURGLASS = 0.1
PENALTY = 4.0
REACH = 1.0


def shifted(value, axis, steps):
    count = lax.axis_size(axis)
    pairs = [(source, (source + steps) % count) for source in range(count)]
    return lax.ppermute(value, axis, pairs)


def inner_rows(first_vec, second_vec):
    return (
        first_vec[0] * second_vec[0] + first_vec[1] * second_vec[1] + first_vec[2] * second_vec[2]
    )


def cross_rows(first_vec, second_vec):
    return jnp.stack(
        [
            first_vec[1] * second_vec[2] - first_vec[2] * second_vec[1],
            first_vec[2] * second_vec[0] - first_vec[0] * second_vec[2],
            first_vec[0] * second_vec[1] - first_vec[1] * second_vec[0],
        ]
    )


def shell_forces(corner_pos, corner_vel, stress_old):
    diag_a = corner_pos[2] - corner_pos[0]
    diag_b = corner_pos[3] - corner_pos[1]
    normal = cross_rows(diag_a, diag_b)
    jacobian = jnp.sqrt(inner_rows(normal, normal))
    axis_three = normal / jacobian
    tangent = diag_a - diag_b
    tangent = tangent - inner_rows(tangent, axis_three) * axis_three
    axis_one = tangent / jnp.sqrt(inner_rows(tangent, tangent))
    axis_two = cross_rows(axis_three, axis_one)
    along_a = inner_rows(diag_a, axis_one)
    across_a = inner_rows(diag_a, axis_two)
    along_b = inner_rows(diag_b, axis_one)
    across_b = inner_rows(diag_b, axis_two)
    speed_a = corner_vel[2] - corner_vel[0]
    speed_b = corner_vel[3] - corner_vel[1]
    slide_a = inner_rows(speed_a, axis_one)
    lift_a = inner_rows(speed_a, axis_two)
    slide_b = inner_rows(speed_b, axis_one)
    lift_b = inner_rows(speed_b, axis_two)
    rate_xx = (across_b * slide_a - across_a * slide_b) / jacobian
    rate_yy = (along_a * lift_b - along_b * lift_a) / jacobian
    rate_xy = (
        across_b * lift_a - across_a * lift_b + along_a * slide_b - along_b * slide_a
    ) / jacobian
    stress_xx = stress_old[0] + DT * STIFF * (rate_xx + POISSON * rate_yy)
    stress_yy = stress_old[1] + DT * STIFF * (POISSON * rate_xx + rate_yy)
    stress_xy = stress_old[2] + DT * STIFF * (0.5 * (1.0 - POISSON)) * rate_xy
    grad_x = (-across_b, across_a, across_b, -across_a)
    grad_y = (along_b, -along_a, -along_b, along_a)
    mode_signs = (1.0, -1.0, 1.0, -1.0)
    twist_mode = corner_vel[0] - corner_vel[1] + corner_vel[2] - corner_vel[3]
    results = []
    for corner_index in range(4):
        force_x = 0.5 * (grad_x[corner_index] * stress_xx + grad_y[corner_index] * stress_xy)
        force_y = 0.5 * (grad_x[corner_index] * stress_xy + grad_y[corner_index] * stress_yy)
        results.append(
            force_x * axis_one
            + force_y * axis_two
            + HOURGLASS * mode_signs[corner_index] * twist_mode
        )
    return (jnp.stack(results), jnp.stack([stress_xx, stress_yy, stress_xy]))


def tile_forces(canonical, pair_rows, flag_rows, rounds):
    per_round = pair_rows.shape[1] // rounds

    def tile_round(round_index, totals):
        start_row = round_index * per_round
        chosen = lax.dynamic_slice_in_dim(pair_rows, start_row, per_round, 1)
        active = lax.dynamic_slice_in_dim(flag_rows, start_row, per_round, 0).astype(jnp.float32)
        near_side = canonical[:, chosen[0], :]
        far_side = canonical[:, chosen[1], :]
        offsets = near_side[:, :, :, None] - far_side[:, :, None, :]
        distance = jnp.sum(offsets * offsets, 0)
        weight = PENALTY * active[:, None, None] * jnp.maximum(REACH - distance, 0.0)
        push_force = weight[None] * offsets
        totals = totals.at[:, chosen[0], :].add(jnp.sum(push_force, 3))
        totals = totals.at[:, chosen[1], :].add(-jnp.sum(push_force, 2))
        return totals

    return lax.fori_loop(0, rounds, tile_round, jnp.zeros_like(canonical))


def local(
    positions,
    velocity,
    mass,
    stress,
    corner_block,
    corner_slot,
    halo_block,
    contact_owner,
    contact_slot,
    tile_pairs,
    tile_active,
):
    blocks_dev = corner_block.shape[2]
    node_state = jnp.concatenate([positions[0], velocity[0]], 0).reshape(6, blocks_dev, CYCLE)
    first_column = halo_block[0, 0]
    rim_state = lax.dynamic_index_in_dim(node_state, first_column, 1, keepdims=False)
    ghost_state = shifted(rim_state, "dom", -1)
    extended = jnp.concatenate([node_state, ghost_state[:, None, :]], 1)
    per_round = max(1, blocks_dev // 16)
    rounds = blocks_dev // per_round
    levels = lax.broadcasted_iota(jnp.int32, (1, 1, CYCLE, 1), 2)

    def element_round(round_index, carried):
        internal, stress_out = carried
        start_row = round_index * per_round
        block_ids = lax.dynamic_slice_in_dim(corner_block[0], start_row, per_round, 1)
        slot_ids = lax.dynamic_slice_in_dim(
            corner_slot[0], start_row * CYCLE, per_round * CYCLE, 1
        ).reshape(4, per_round, CYCLE)
        stress_here = lax.dynamic_slice_in_dim(stress[0], start_row * CYCLE, per_round * CYCLE, 1)
        picked = extended[:, block_ids, :]
        onehot = (slot_ids[:, :, None, :] == levels).astype(jnp.float32)
        corner = jnp.einsum("rcpk,cpki->crpi", picked, onehot, precision=lax.Precision.HIGHEST)
        corner = corner.reshape(4, 6, per_round * CYCLE)
        forces, stress_new = shell_forces(corner[:, :3], corner[:, 3:], stress_here)
        spread = jnp.einsum(
            "cxpi,cpki->xcpk",
            forces.reshape(4, 3, per_round, CYCLE),
            onehot,
            precision=lax.Precision.HIGHEST,
        )
        internal = internal.at[:, block_ids, :].add(spread)
        stress_out = lax.dynamic_update_slice_in_dim(stress_out, stress_new, start_row * CYCLE, 1)
        return (internal, stress_out)

    internal, stress_next = lax.fori_loop(
        0,
        rounds,
        element_round,
        (jnp.zeros((3, blocks_dev + 1, CYCLE), jnp.float32), jnp.zeros_like(stress[0])),
    )
    ghost_force = shifted(internal[:, blocks_dev, :], "dom", 1)
    own_force = internal[:, :blocks_dev, :]
    current = lax.dynamic_index_in_dim(own_force, first_column, 1, keepdims=True)
    own_force = lax.dynamic_update_index_in_dim(
        own_force, current + ghost_force[:, None, :], first_column, 1
    )
    groups = lax.axis_size("group")
    dom_count = lax.axis_size("dom")
    capacity = tile_pairs.shape[2] // (groups - 1)
    tile_rounds = math.gcd(capacity, 8)
    owner_index = contact_owner[0]
    slot_index = contact_slot[0]
    is_live = owner_index >= 0
    owner_safe = jnp.maximum(owner_index, 0)
    spot_index = jnp.maximum(slot_index, 0) % capacity
    block_pos = positions[0].reshape(3, blocks_dev, CYCLE)
    devices = groups * dom_count
    target = jnp.where(is_live, owner_index, devices)
    outgoing = (
        jnp.zeros((3, devices, capacity, CYCLE), jnp.float32)
        .at[:, target, spot_index, :]
        .set(block_pos, mode="drop")
    )
    arrived = lax.all_to_all(outgoing, ("group", "dom"), split_axis=1, concat_axis=1, tiled=True)
    canonical = jnp.sum(arrived.reshape(3, groups, dom_count, capacity, CYCLE), 2).reshape(
        3, groups * capacity, CYCLE
    )
    owner_force = tile_forces(canonical, tile_pairs[0], tile_active[0], tile_rounds)
    answer = jnp.broadcast_to(
        owner_force.reshape(3, groups, 1, capacity, CYCLE), (3, groups, dom_count, capacity, CYCLE)
    ).reshape(3, devices, capacity, CYCLE)
    returned = lax.all_to_all(answer, ("group", "dom"), split_axis=1, concat_axis=1, tiled=True)
    contact = returned[:, owner_safe, spot_index, :]
    contact = jnp.where(is_live[None, :, None], contact, 0.0)
    velocity_next = (
        velocity[0] + DT * (contact.reshape(3, -1) - own_force.reshape(3, -1)) / mass[0][None, :]
    )
    return (velocity_next[None], stress_next[None])


def solution(mesh):
    in_specs = (
        P("group", None, "dom"),
        P("group", None, "dom"),
        P("group", "dom"),
        P("group", None, "dom"),
        P("group", None, "dom"),
        P("group", None, "dom"),
        P("group", "dom"),
        P("group", "dom"),
        P("group", "dom"),
        P("group", None, "dom"),
        P("group", "dom"),
    )
    out_specs = (P("group", None, "dom"), P("group", None, "dom"))
    return jax.shard_map(local, mesh=mesh, in_specs=in_specs, out_specs=out_specs, check_vma=False)
```

profile of v0, /device:TPU:0, one launch (start us, length us, event | category | flops | bytes accessed | tf_op | source)
XLA Modules:
  0.0 194.8 jit_solution(11740885044239158754)
XLA Ops:
  2.0 1.0 copy.59
  3.5 3.2 %scatter_fusion.3 = f32[3,128,8,128]{3,0,2,1:T(4,128)S(1)} fusion(f32[3,128,8,128]{3,0,2,1:T(4,128)S(1)} %broadcast_in_dim.115, s32[64]{0:T(128)S(1)} %fusion.40, f32[64,3,128]{2,1,0:T(4,128)S(1)} %copy.59), kind=kCustom, calls=%fused_computation.7 | custom fusion | bytes 295424 | tf_op jit(solution)/shard_map/scatter | solution.py:178
  6.7 1.3 copy.60
  8.0 11.1 %all-to-all-start = ((f32[3,128,8,128]{3,2,0,1:T(8,128)}), f32[3,128,8,128]{3,2,0,1:T(8,128)S(1)}, u32[]{:S(2)}, u32[]{:S(2)}) async-start(f32[3,128,8,128]{3,2,0,1:T(8,128)} %copy.60), calls=%async_computation | async-start | bytes 3145728 | tf_op jit(solution)/shard_map/all_to_all | solution.py:180
  19.9 4.2 %collective-permute-start = (f32[6,128]{1,0:T(8,128)S(1)}, f32[6,128]{1,0:T(8,128)S(1)}, u32[]{:S(2)}, u32[]{:S(2)}) collective-permute-start(f32[6,128]{1,0:T(8,128)S(1)} %bitcast.393), channel_id=1, source_target_pairs={{0,31},{1,0},{2,1},{3,2},{4,3},{5,4},{6,5},{7,6},{8,7},{9,8},{10,9... | collective-permute-start | bytes 9224 | tf_op jit(solution)/shard_map/ppermute | solution.py:22
  24.1 8.9 %collective-permute-done = f32[6,128]{1,0:T(8,128)S(1)} collective-permute-done((f32[6,128]{1,0:T(8,128)S(1)}, f32[6,128]{1,0:T(8,128)S(1)}, u32[]{:S(2)}, u32[]{:S(2)}) %collective-permute-start) | collective-permute-done | bytes 3104 | tf_op jit(solution)/shard_map/ppermute | solution.py:22
  33.1 10.8 %all-to-all-done = f32[3,128,8,128]{3,2,0,1:T(8,128)S(1)} async-done(((f32[3,128,8,128]{3,2,0,1:T(8,128)}), f32[3,128,8,128]{3,2,0,1:T(8,128)S(1)}, u32[]{:S(2)}, u32[]{:S(2)}) %all-to-all-start) | async-done | bytes 1572896 | tf_op jit(solution)/shard_map/all_to_all | solution.py:180
  44.1 27.5 %while.31 = (s32[]{:T(128)}, f32[3,32,128]{2,0,1:T(4,128)S(1)}, s32[2,24]{1,0:T(2,128)S(1)}, s32[24]{0:T(128)S(1)}, f32[3,32,128]{2,0,1:T(4,128)S(1)}, /*index=5*/s32[]{:T(128)}, s32[]{:T(128)}, s32[]{:T(128)}, s32[]{:T(128)}) while((s32[]{:T(128)}, f32[3,32,128]{2,0,1:T(4,128)S(1)}, s32[2,24]{1,0:T(2,128)S(1)}, s32[24]{0:T(128)S(1)}, ...), condition=%wide.region_8.9_spmd, body=%wide.region_2.8_spmd.sunk | while | flops 1133726 | bytes 914791 | solution.py:102
  71.6 1.3 broadcast_in_dim.118
  72.8 4.8 %all-to-all-start.1 = ((f32[3,128,8,128]{3,2,0,1:T(8,128)}), f32[3,128,8,128]{3,2,0,1:T(8,128)S(1)}, u32[]{:S(2)}, u32[]{:S(2)}) async-start(f32[3,128,8,128]{3,2,0,1:T(8,128)} %bitcast.20), calls=%async_computation.1 | async-start | bytes 3145728 | tf_op jit(solution)/shard_map/all_to_all | solution.py:188
  77.7 105.6 %while.32 = (s32[]{:T(128)}, f32[3,65,128]{2,0,1:T(4,128)S(1)}, f32[3,8192]{1,0:T(4,128)S(1)}, s32[1,4,64]{2,1,0:T(4,128)S(1)}, s32[1,4,8192]{2,1,0:T(4,128)}, /...) while((s32[]{:T(128)}, f32[3,65,128]{2,0,1:T(4,128)S(1)}, ...), condition=%wide.region_11.12_spmd.clone, body=%wide.region_9.11_spmd.clone.sunk | while | flops 29005368 | bytes 830189 | solution.py:151
  79.9 0.7 multiply_add_fusion.22
  82.2 0.9 fusion.64
  83.1 1.1 scatter_fusion.2
  86.5 0.7 multiply_add_fusion.22
  88.8 0.9 fusion.64
  89.7 1.1 scatter_fusion.2
  95.4 0.9 fusion.64
  96.3 1.1 scatter_fusion.2
  102.0 0.9 fusion.64
  102.9 1.1 scatter_fusion.2
  108.6 0.9 fusion.64
  109.5 1.1 scatter_fusion.2
  115.2 0.9 fusion.64
  116.1 1.1 scatter_fusion.2
  121.8 0.9 fusion.64
  122.7 1.1 scatter_fusion.2
  128.4 0.9 fusion.64
  129.3 1.1 scatter_fusion.2
  135.0 0.9 fusion.64
  135.9 1.1 scatter_fusion.2
  141.6 0.9 fusion.64
  142.5 1.1 scatter_fusion.2
  148.2 0.9 fusion.64
  149.1 1.1 scatter_fusion.2
  154.8 0.9 fusion.64
  155.7 1.1 scatter_fusion.2
  161.4 0.9 fusion.64
  162.3 1.1 scatter_fusion.2
  168.0 0.9 fusion.64
  168.9 1.1 scatter_fusion.2
  174.6 0.9 fusion.64
  175.5 1.1 scatter_fusion.2
  181.2 0.9 fusion.64
  182.1 1.1 scatter_fusion.2
  184.2 5.5 %collective-permute-done.1 = f32[3,128]{1,0:T(4,128)S(1)} collective-permute-done((f32[3,128]{1,0:T(4,128)S(1)}, f32[3,128]{1,0:T(4,128)S(1)}, u32[]{:S(2)}, u32[]{:S(2)}) %collective-permute-start.1) | collective-permute-done | bytes 1568 | tf_op jit(solution)/shard_map/ppermute | solution.py:22
  189.7 1.9 copy.64
  191.6 2.3 %gather_fusion.3 = f32[64,3,128]{2,1,0:T(4,128)S(1)} fusion(f32[3,128,8,128]{3,0,2,1:T(4,128)} %copy.64, s32[64]{0:T(128)S(1)} %get-tuple-element.426), kind=kCustom, calls=%fused_computation.3 | custom fusion | bytes 197120 | tf_op jit(solution)/shard_map/gather | solution.py:189
  (501 shorter events, 100.3 us)
Async XLA Ops:
  8.0 11.8 %copy-start = (f32[1,3,8192]{2,0,1:T(1,128)S(1)}, f32[1,3,8192]{2,0,1:T(1,128)}, u32[]{:S(2)}) copy-start(f32[1,3,8192]{2,0,1:T(1,128)} %param.15) | copy-start | bytes 294916
  8.0 11.9 %copy-start.1 = (f32[1,3,8192]{2,0,1:T(1,128)S(1)}, f32[1,3,8192]{2,0,1:T(1,128)}, u32[]{:S(2)}) copy-start(f32[1,3,8192]{2,0,1:T(1,128)} %param.16) | copy-start | bytes 294916
  8.0 16.1 %copy-start.5 = (s32[1,64]{1,0:T(1,128)S(1)}, s32[1,64]{1,0:T(1,128)}, u32[]{:S(2)}) copy-start(s32[1,64]{1,0:T(1,128)} %param.22) | copy-start | bytes 772
  8.0 35.9 %all-to-all-start = ((f32[3,128,8,128]{3,2,0,1:T(8,128)}), f32[3,128,8,128]{3,2,0,1:T(8,128)S(1)}, u32[]{:S(2)}, u32[]{:S(2)}) async-start(f32[3,128,8,128]{3,2,0,1:T(8,128)} %copy.60), calls=%async_computation | async-start | bytes 3145728 | tf_op jit(solution)/shard_map/all_to_all | solution.py:180
  19.2 24.9 %copy-start.4 = (s32[1,2,24]{2,1,0:T(2,128)S(1)}, s32[1,2,24]{2,1,0:T(2,128)}, u32[]{:S(2)}) copy-start(s32[1,2,24]{2,1,0:T(2,128)} %param.24) | copy-start | bytes 580
  19.2 24.9 %copy-start.6 = (s32[1,24]{1,0:T(1,128)S(1)}, s32[1,24]{1,0:T(1,128)}, u32[]{:S(2)}) copy-start(s32[1,24]{1,0:T(1,128)} %param.25) | copy-start | bytes 292
  19.9 13.1 %collective-permute-start = (f32[6,128]{1,0:T(8,128)S(1)}, f32[6,128]{1,0:T(8,128)S(1)}, u32[]{:S(2)}, u32[]{:S(2)}) collective-permute-start(f32[6,128]{1,0:T(8,128)S(1)} %bitcast.393), channel_id=1, source_target_pairs={{0,31},{1,0},{2,1},{3,2},{4,3},{5,4},{6,5},{7,6},{8,7},{9,8},{10,9... | collective-permute-start | bytes 9224 | tf_op jit(solution)/shard_map/ppermute | solution.py:22
  72.8 4.8 %copy-start.2 = (s32[1,4,64]{2,1,0:T(4,128)S(1)}, s32[1,4,64]{2,1,0:T(4,128)}, u32[]{:S(2)}) copy-start(s32[1,4,64]{2,1,0:T(4,128)} %param.19) | copy-start | bytes 3076
  72.8 116.8 %all-to-all-start.1 = ((f32[3,128,8,128]{3,2,0,1:T(8,128)}), f32[3,128,8,128]{3,2,0,1:T(8,128)S(1)}, u32[]{:S(2)}, u32[]{:S(2)}) async-start(f32[3,128,8,128]{3,2,0,1:T(8,128)} %bitcast.20), calls=%async_computation.1 | async-start | bytes 3145728 | tf_op jit(solution)/shard_map/all_to_all | solution.py:188
  183.3 6.4 %collective-permute-start.1 = (f32[3,128]{1,0:T(4,128)S(1)}, f32[3,128]{1,0:T(4,128)S(1)}, u32[]{:S(2)}, u32[]{:S(2)}) collective-permute-start(f32[3,128]{1,0:T(4,128)S(1)} %slice_bitcast_fusion.15), channel_id=1, source_target_pairs={{0,1},{1,2},{2,3},{3,4},{4,5},{5,6},{6,7},{7,8},{8,9},{9,10},{10,1... | collective-permute-start | bytes 4616 | tf_op jit(solution)/shard_map/ppermute | solution.py:22
  183.4 10.5 %copy-start.3 = (f32[1,8192]{1,0:T(1,128)S(1)}, f32[1,8192]{1,0:T(1,128)}, u32[]{:S(2)}) copy-start(f32[1,8192]{1,0:T(1,128)} %param.17) | copy-start | bytes 98308
where the time goes:
time: 197 us; the launch traced here: 195 us
  other arithmetic  76.9 us (39%)
  local copies, waits for them, and re-layouts  45 us (23%)
  waiting for transfers between devices  25.2 us (13%)
  matrix products  23.6 us (12%)
  starting transfers between devices  20.2 us (10%)
  loops' own time  2.44 us (1%)
    scatter-add x16, other arithmetic, element_round(): internal = internal.at[:, block_ids, :].add(spread)  18.3 us
    dot_general x16, matrix products, element_round(): jnp.einsum('cxpi,cpki->xcpk', forces.reshape(4, 3, per_round, CYCLE), one...  14.5 us
    ppermute x2, waiting for transfers between devices, shifted(): return lax.ppermute(value, axis, pairs)  14.4 us
    mul x32, other arithmetic, shell_forces(): 0.5 * (grad_x[corner_index] * stress_xx + grad_y[corner_index] * stress_xy)  12.2 us
    add x16, other arithmetic, shell_forces(): stress_xy = stress_old[2] + DT * STIFF * (0.5 * (1.0 - POISSON)) * rate_xy  11.9 us
    mul x16, other arithmetic, shell_forces(): 0.5 * (grad_x[corner_index] * stress_xy + grad_y[corner_index] * stress_yy)  11.2 us
    dynamic_slice x16, local copies, waits for them, and re-layouts, element_round(): lax.dynamic_slice_in_dim(corner_slot[0], start_row * CYCLE, per_round * C...  11.2 us
    all_to_all x1, starting transfers between devices, local(): lax.all_to_all(outgoing, ('group', 'dom'), split_axis=1, concat_axis=1, t...  11.1 us
  transfers between devices with their start and end apart: 4, of which 3 were waited for; matrix products, arithmetic and copies ran while one was open for 54% of the time, Pallas kernels for 0%

commit v1 on v0

v1 whole, which is shorter than its diff:
```python
import functools

import jax
import jax.numpy as jnp
from jax import lax
from jax.experimental import pallas as pl
from jax.experimental.pallas import tpu as pltpu
from jax.sharding import PartitionSpec as P

LANES = 128
ROWS = 8
DT = 0.5
STIFF = 2.0
POISSON = 0.3
HOURGLASS = 0.1
PENALTY = 4.0
REACH = 1.0
MESH = pl.DeviceIdType.MESH
HIGHEST = lax.Precision.HIGHEST


def inner_rows(a, b):
    return a[0] * b[0] + a[1] * b[1] + a[2] * b[2]


def cross_rows(a, b):
    return (
        a[1] * b[2] - a[2] * b[1],
        a[2] * b[0] - a[0] * b[2],
        a[0] * b[1] - a[1] * b[0],
    )


def minus(a, b):
    return tuple(x - y for x, y in zip(a, b))


def scaled(a, s):
    return tuple(x * s for x in a)


def shell_forces(pos, vel, stress_old):
    diag_a = minus(pos[2], pos[0])
    diag_b = minus(pos[3], pos[1])
    normal = cross_rows(diag_a, diag_b)
    inv_j = lax.rsqrt(inner_rows(normal, normal))
    axis_three = scaled(normal, inv_j)
    tangent = minus(diag_a, diag_b)
    tangent = minus(tangent, scaled(axis_three, inner_rows(tangent, axis_three)))
    axis_one = scaled(tangent, lax.rsqrt(inner_rows(tangent, tangent)))
    axis_two = cross_rows(axis_three, axis_one)
    along_a = inner_rows(diag_a, axis_one)
    across_a = inner_rows(diag_a, axis_two)
    along_b = inner_rows(diag_b, axis_one)
    across_b = inner_rows(diag_b, axis_two)
    speed_a = minus(vel[2], vel[0])
    speed_b = minus(vel[3], vel[1])
    slide_a = inner_rows(speed_a, axis_one)
    lift_a = inner_rows(speed_a, axis_two)
    slide_b = inner_rows(speed_b, axis_one)
    lift_b = inner_rows(speed_b, axis_two)
    rate_xx = (across_b * slide_a - across_a * slide_b) * inv_j
    rate_yy = (along_a * lift_b - along_b * lift_a) * inv_j
    rate_xy = (
        across_b * lift_a - across_a * lift_b + along_a * slide_b - along_b * slide_a
    ) * inv_j
    s_xx = stress_old[0] + (DT * STIFF) * (rate_xx + POISSON * rate_yy)
    s_yy = stress_old[1] + (DT * STIFF) * (POISSON * rate_xx + rate_yy)
    s_xy = stress_old[2] + (DT * STIFF * 0.5 * (1.0 - POISSON)) * rate_xy
    half_xx, half_yy, half_xy = 0.5 * s_xx, 0.5 * s_yy, 0.5 * s_xy
    fx0 = along_b * half_xy - across_b * half_xx
    fy0 = along_b * half_yy - across_b * half_xy
    fx1 = across_a * half_xx - along_a * half_xy
    fy1 = across_a * half_xy - along_a * half_yy
    forces = [[], [], [], []]
    for c in range(3):
        mode = HOURGLASS * (vel[0][c] - vel[1][c] + vel[2][c] - vel[3][c])
        first = fx0 * axis_one[c] + fy0 * axis_two[c]
        second = fx1 * axis_one[c] + fy1 * axis_two[c]
        forces[0].append(mode + first)
        forces[1].append(second - mode)
        forces[2].append(mode - first)
        forces[3].append(-mode - second)
    return forces, (s_xx, s_yy, s_xy)


def kernel(
    groups,
    doms,
    pos_ref,
    vel_ref,
    mass_ref,
    stress_ref,
    slot_ref,
    cb_ref,
    owner_ref,
    spot_ref,
    pair_ref,
    cb_smem,
    halo_smem,
    pair_smem,
    active_smem,
    vel_out,
    stress_out,
    state,
    rim,
    ghost_in,
    out_buf,
    in_buf,
    ans,
    ret,
    canon,
    tile_out,
    inverse,
    corner_buf,
    force_buf,
    spread,
    push_out,
    push_in,
    fwd_send,
    fwd_recv,
    back_send,
    back_recv,
    rim_sems,
    push_sems,
):
    g = lax.axis_index("group")
    d = lax.axis_index("dom")
    blocks = mass_ref.shape[0]
    tiles = pair_ref.shape[1]
    slots = groups * ROWS
    left = lax.rem(d + doms - 1, doms)
    right = lax.rem(d + 1, doms)
    partners = []
    for turn in range(groups):
        k = lax.rem(g + turn, groups)
        for step, dd in ((0, left), (1, d), (2, right)):
            if turn == 0 and step == 1:
                continue
            partners.append((turn, k, step, dd))

    barrier = pltpu.get_barrier_semaphore()
    for turn, k, step, dd in partners:
        pl.semaphore_signal(barrier, inc=1, device_id=(k, dd), device_id_type=MESH)

    halo = halo_smem[0, 0]
    state_rows = state.reshape((blocks + 1) * ROWS, LANES)
    for c in range(3):
        state_rows[pl.ds(c, blocks, stride=ROWS), :] = pos_ref[c]
        state_rows[pl.ds(3 + c, blocks, stride=ROWS), :] = vel_ref[c]
    rim[...] = state[halo]

    owner = owner_ref[...]
    step_of = lax.rem(lax.rem(owner, doms) - d + 1 + doms, doms)
    goal = (lax.div(owner, doms) * 3 + step_of) * ROWS + lax.rem(spot_ref[...], ROWS)
    goal = jnp.where(owner >= 0, goal, -1)
    places = groups * 3 * ROWS
    chosen = (
        lax.broadcasted_iota(jnp.int32, (places, blocks), 0) == goal
    ).astype(jnp.float32)
    for c in range(3):
        column = pos_ref[c]
        packed = jnp.dot(chosen, column, precision=HIGHEST, preferred_element_type=jnp.float32)
        out_buf[:, :, c, :, :] = packed.reshape(groups, 3, ROWS, LANES)

    pl.semaphore_wait(barrier, len(partners))

    rim_copy = pltpu.make_async_remote_copy(
        src_ref=rim,
        dst_ref=ghost_in,
        send_sem=rim_sems.at[0],
        recv_sem=rim_sems.at[1],
        device_id=(g, left),
        device_id_type=MESH,
    )
    rim_copy.start()
    forward = []
    for turn, k, step, dd in partners:
        copy = pltpu.make_async_remote_copy(
            src_ref=out_buf.at[k, step],
            dst_ref=in_buf.at[step, g],
            send_sem=fwd_send.at[turn, step],
            recv_sem=fwd_recv.at[turn, step],
            device_id=(k, dd),
            device_id_type=MESH,
        )
        copy.start()
        forward.append(copy)
    in_buf[1, g] = out_buf[g, 1]

    lane16 = lax.broadcasted_iota(jnp.int32, (16, 2 * LANES), 1)
    row16 = lax.broadcasted_iota(jnp.int32, (16, 2 * LANES), 0)
    half = lax.div(lane16, LANES)
    weights = jnp.where(lax.rem(lax.div(row16, 4), 2) == half, lax.rem(lane16, LANES), 0)
    weights = weights.astype(jnp.float32).astype(jnp.bfloat16)
    rows_of = lax.broadcasted_iota(jnp.int32, (16, LANES), 0)
    one = jnp.ones((16, LANES), jnp.bfloat16)
    zero = jnp.zeros((16, LANES), jnp.bfloat16)

    def invert(k, carry):
        ids = slot_ref[:, pl.ds(pl.multiple_of(k * LANES, LANES), LANES)].astype(jnp.float32)
        level = [
            (rows_of + 16 * j).astype(jnp.float32).astype(jnp.bfloat16) for j in range(ROWS)
        ]
        marks = []
        for c in range(4):
            here = jnp.broadcast_to(ids[c : c + 1, :], (16, LANES)).astype(jnp.bfloat16)
            marks.append(
                jnp.concatenate([jnp.where(here == lv, one, zero) for lv in level], 0)
            )
        for side, (first, second) in enumerate(((0, 3), (1, 2))):
            both = jnp.concatenate([marks[first], marks[second]], 1)
            found = lax.dot_general(
                weights, both, (((1,), (1,)), ((), ())), preferred_element_type=jnp.float32
            )
            inverse[side, k] = found[0:ROWS, :].astype(jnp.int32)
        return carry

    lax.fori_loop(0, blocks, invert, 0, unroll=2)

    for copy in forward:
        copy.wait_recv()
    canon_rows = canon.reshape(slots * ROWS, LANES)
    for c in range(3):
        for layer in range(groups):
            canon_rows[pl.ds(layer * ROWS * ROWS + c, ROWS, stride=ROWS), :] = (
                in_buf[0, layer, c] + in_buf[1, layer, c] + in_buf[2, layer, c]
            )
    sub_iota = lax.broadcasted_iota(jnp.int32, (ROWS, LANES), 0)
    lane_iota = lax.broadcasted_iota(jnp.int32, (ROWS, LANES), 1)

    def one_tile(t, carry):
        i = pair_smem[0, t]
        j = pair_smem[1, t]
        gain = PENALTY * active_smem[0, t].astype(jnp.float32)
        near_block = canon[i]
        far_block = canon[j]
        near = [jnp.broadcast_to(near_block[c : c + 1, :], (ROWS, LANES)) for c in range(3)]
        far = [jnp.broadcast_to(far_block[c : c + 1, :], (ROWS, LANES)) for c in range(3)]
        near_sum = [jnp.zeros((ROWS, LANES), jnp.float32) for _ in range(3)]
        far_sum = [jnp.zeros((ROWS, LANES), jnp.float32) for _ in range(3)]
        for r in range(LANES // ROWS):
            at = sub_iota + ROWS * r
            diff = [
                jnp.take_along_axis(near[c], at, axis=1, mode="promise_in_bounds") - far[c]
                for c in range(3)
            ]
            weight = gain * jnp.maximum(REACH - inner_rows(diff, diff), 0.0)
            for c in range(3):
                push = weight * diff[c]
                far_sum[c] = far_sum[c] + push
                total = jnp.sum(push, 1, keepdims=True)
                near_sum[c] = jnp.where(lane_iota == at, total, near_sum[c])
        for c in range(3):
            tile_out[c, pl.ds(t, 1), :] = jnp.sum(
                jnp.where(lax.rem(lane_iota, ROWS) == sub_iota, near_sum[c], 0.0),
                0,
                keepdims=True,
            )
            tile_out[c, pl.ds(tiles + t, 1), :] = jnp.sum(far_sum[c], 0, keepdims=True)
        return carry

    lax.fori_loop(0, tiles, one_tile, 0)
    slot_iota = lax.broadcasted_iota(jnp.int32, (slots, tiles), 0)
    take_near = (slot_iota == pair_ref[0:1, :]).astype(jnp.float32)
    take_far = (slot_iota == pair_ref[1:2, :]).astype(jnp.float32)
    for c in range(3):
        total = jnp.dot(
            take_near, tile_out[c, 0:tiles, :], precision=HIGHEST, preferred_element_type=jnp.float32
        ) - jnp.dot(
            take_far,
            tile_out[c, tiles : 2 * tiles, :],
            precision=HIGHEST,
            preferred_element_type=jnp.float32,
        )
        ans[:, c, :, :] = total.reshape(groups, ROWS, LANES)
    backward = []
    for turn, k, step, dd in partners:
        copy = pltpu.make_async_remote_copy(
            src_ref=ans.at[k],
            dst_ref=ret.at[g, 2 - step],
            send_sem=back_send.at[turn, step],
            recv_sem=back_recv.at[turn, step],
            device_id=(k, dd),
            device_id_type=MESH,
        )
        copy.start()
        backward.append(copy)
    ret[g, 1] = ans[g]

    rim_copy.wait_recv()
    state[blocks] = ghost_in[...]

    def elements(part, carry):
        for kk in range(ROWS):
            k = part * ROWS + kk
            at = pl.ds(pl.multiple_of(k * LANES, LANES), LANES)
            ids = slot_ref[:, at]
            for side, pair in enumerate(((0, 3), (1, 2))):
                b = cb_smem[side, k]
                block = state[b]
                for c in pair:
                    index = jnp.broadcast_to(ids[c : c + 1, :], (ROWS, LANES))
                    corner_buf[c, pl.ds(kk * ROWS, ROWS), :] = jnp.take_along_axis(
                        block, index, axis=1, mode="promise_in_bounds"
                    )
        pos = [[corner_buf[c, pl.ds(x, ROWS, stride=ROWS), :] for x in range(3)] for c in range(4)]
        vel = [
            [corner_buf[c, pl.ds(3 + x, ROWS, stride=ROWS), :] for x in range(3)] for c in range(4)
        ]
        here = pl.ds(pl.multiple_of(part * ROWS, ROWS), ROWS)
        old = [stress_ref[x, here, :] for x in range(3)]
        forces, new = shell_forces(pos, vel, old)
        for x in range(3):
            stress_out[x, here, :] = new[x]
            force_buf[0, pl.ds(x, ROWS, stride=ROWS), :] = forces[0][x]
            force_buf[0, pl.ds(4 + x, ROWS, stride=ROWS), :] = forces[3][x]
            force_buf[1, pl.ds(x, ROWS, stride=ROWS), :] = forces[1][x]
            force_buf[1, pl.ds(4 + x, ROWS, stride=ROWS), :] = forces[2][x]
        for kk in range(ROWS):
            k = part * ROWS + kk
            for side in range(2):
                spread[side, pl.ds(pl.multiple_of(k * ROWS, ROWS), ROWS), :] = jnp.take_along_axis(
                    force_buf[side, pl.ds(kk * ROWS, ROWS), :],
                    inverse[side, k],
                    axis=1,
                    mode="promise_in_bounds",
                )
        return carry

    lax.fori_loop(0, blocks // ROWS, elements, 0)

    block_iota = lax.broadcasted_iota(jnp.int32, (blocks + ROWS, blocks), 0)
    hits = [(block_iota == cb_ref[side : side + 1, :]).astype(jnp.float32) for side in range(2)]
    internal = []
    for c in range(3):
        total = None
        for side in range(2):
            part = (
                spread[side, pl.ds(c, blocks, stride=ROWS), :]
                + spread[side, pl.ds(4 + c, blocks, stride=ROWS), :]
            )
            value = jnp.dot(
                hits[side], part, precision=HIGHEST, preferred_element_type=jnp.float32
            )
            total = value if total is None else total + value
        internal.append(total)
        push_out[pl.ds(c, 1), :] = total[blocks : blocks + 1, :]
    push_copy = pltpu.make_async_remote_copy(
        src_ref=push_out,
        dst_ref=push_in,
        send_sem=push_sems.at[0],
        recv_sem=push_sems.at[1],
        device_id=(g, right),
        device_id_type=MESH,
    )
    push_copy.start()

    for copy in backward:
        copy.wait_recv()
    contact = []
    for c in range(3):
        answers = ret[:, :, c, :, :].reshape(places, LANES)
        contact.append(
            lax.dot_general(
                chosen,
                answers,
                (((0,), (0,)), ((), ())),
                precision=HIGHEST,
                preferred_element_type=jnp.float32,
            )
        )
    push_copy.wait_recv()
    is_rim = lax.broadcasted_iota(jnp.int32, (blocks, LANES), 0) == halo
    factor = DT / mass_ref[...]
    for c in range(3):
        extra = jnp.where(is_rim, push_in[pl.ds(c, 1), :], 0.0)
        force = contact[c] - internal[c][0:blocks, :] - extra
        vel_out[c] = vel_ref[c] + factor * force
    rim_copy.wait_send()
    push_copy.wait_send()
    for copy in forward:
        copy.wait_send()
    for copy in backward:
        copy.wait_send()


def local(
    positions,
    velocity,
    mass,
    stress,
    corner_block,
    corner_slot,
    halo_block,
    contact_owner,
    contact_slot,
    tile_pairs,
    tile_active,
):
    groups = lax.axis_size("group")
    doms = lax.axis_size("dom")
    blocks = corner_block.shape[2]
    nodes = positions.shape[2]
    tiles = tile_pairs.shape[2]
    slots = groups * ROWS
    vmem = pl.BlockSpec(memory_space=pltpu.VMEM)
    smem = pl.BlockSpec(memory_space=pltpu.SMEM)
    f32 = jnp.float32
    out = pl.pallas_call(
        functools.partial(kernel, groups, doms),
        out_shape=[jax.ShapeDtypeStruct((3, blocks, LANES), f32)] * 2,
        in_specs=[vmem] * 9 + [smem] * 4,
        out_specs=[vmem] * 2,
        scratch_shapes=[
            pltpu.VMEM((blocks + 1, ROWS, LANES), f32),
            pltpu.VMEM((ROWS, LANES), f32),
            pltpu.VMEM((ROWS, LANES), f32),
            pltpu.VMEM((groups, 3, 3, ROWS, LANES), f32),
            pltpu.VMEM((3, groups, 3, ROWS, LANES), f32),
            pltpu.VMEM((groups, 3, ROWS, LANES), f32),
            pltpu.VMEM((groups, 3, 3, ROWS, LANES), f32),
            pltpu.VMEM((slots, ROWS, LANES), f32),
            pltpu.VMEM((3, 2 * tiles, LANES), f32),
            pltpu.VMEM((2, blocks, ROWS, LANES), jnp.int32),
            pltpu.VMEM((4, ROWS * ROWS, LANES), f32),
            pltpu.VMEM((2, ROWS * ROWS, LANES), f32),
            pltpu.VMEM((2, blocks * ROWS, LANES), f32),
            pltpu.VMEM((ROWS, LANES), f32),
            pltpu.VMEM((ROWS, LANES), f32),
            pltpu.SemaphoreType.DMA((groups, 3)),
            pltpu.SemaphoreType.DMA((groups, 3)),
            pltpu.SemaphoreType.DMA((groups, 3)),
            pltpu.SemaphoreType.DMA((groups, 3)),
            pltpu.SemaphoreType.DMA((2,)),
            pltpu.SemaphoreType.DMA((2,)),
        ],
        compiler_params=pltpu.CompilerParams(
            collective_id=0, has_side_effects=True, vmem_limit_bytes=32 * 1024 * 1024
        ),
        name="shell_step",
    )(
        positions.reshape(3, blocks, LANES),
        velocity.reshape(3, blocks, LANES),
        mass.reshape(blocks, LANES),
        stress.reshape(3, blocks, LANES),
        corner_slot.reshape(4, nodes),
        corner_block.reshape(4, blocks),
        contact_owner,
        contact_slot,
        tile_pairs.reshape(2, tiles),
        corner_block.reshape(4, blocks),
        halo_block,
        tile_pairs.reshape(2, tiles),
        tile_active,
    )
    return out[0].reshape(1, 3, nodes), out[1].reshape(1, 3, nodes)


def solution(mesh):
    in_specs = (
        P("group", None, "dom"),
        P("group", None, "dom"),
        P("group", "dom"),
        P("group", None, "dom"),
        P("group", None, "dom"),
        P("group", None, "dom"),
        P("group", "dom"),
        P("group", "dom"),
        P("group", "dom"),
        P("group", None, "dom"),
        P("group", "dom"),
    )
    out_specs = (P("group", None, "dom"), P("group", None, "dom"))
    return jax.shard_map(local, mesh=mesh, in_specs=in_specs, out_specs=out_specs, check_vma=False)
```

time: 197 us -> 59.6 us (0.30)
  other arithmetic: 76.9 us -> 0 us
  Pallas kernels: 0 us -> 51.7 us
  local copies, waits for them, and re-layouts: 45 us -> 6.31 us
  waiting for transfers between devices: 25.2 us -> 0 us
  matrix products: 23.6 us -> 0 us
  starting transfers between devices: 20.2 us -> 0 us
  loops' own time: 2.44 us -> 0 us
    pallas_call x0 -> x1, Pallas kernels: none -> 51.7 us  [local(): pl.pallas_call(functools.partial(kernel, groups, doms), out_shape=[jax.Sh...]
    scatter-add x32 -> x0, other arithmetic: 28.6 us -> none  [the longest x16 18.3 us: element_round(): internal = internal.at[:, block_ids, :].add(spread)]
    mul x64 -> x0, other arithmetic: 24.7 us -> none  [the longest x32 12.2 us: shell_forces(): 0.5 * (grad_x[corner_index] * stress_xx + grad_y[corner_index] * stress_xy)]
    dot_general x32 -> x0, matrix products: 23.6 us -> none  [the longest x16 14.5 us: element_round(): jnp.einsum('cxpi,cpki->xcpk', forces.reshape(4, 3, per_round, CYCLE), one...]
    gather x49 -> x0, local copies, waits for them, and re-layouts: 20.6 us -> none  [the longest x16 9.01 us: element_round(): picked = extended[:, block_ids, :]]
    all_to_all x2 -> x0, starting transfers between devices: 15.9 us -> none  [the longest x1 11.1 us: local(): lax.all_to_all(outgoing, ('group', 'dom'), split_axis=1, concat_axis=1, t...]
    ppermute x2 -> x0, waiting for transfers between devices: 14.4 us -> none  [shifted(): return lax.ppermute(value, axis, pairs)]
    add x33 -> x0, other arithmetic: 12.3 us -> none  [the longest x16 11.9 us: shell_forces(): stress_xy = stress_old[2] + DT * STIFF * (0.5 * (1.0 - POISSON)) * rate_xy]
  transfers between devices with their start and end apart: 4 -> 0, of which waited for: 3 -> 0; matrix products, arithmetic and copies ran while one was open for 54% -> 0% of each run, Pallas kernels for 0% -> 0%
where the time goes in v1:
time: 59.6 us; the launch traced here: 59.3 us
  Pallas kernels  51.7 us (87%)
  local copies, waits for them, and re-layouts  6.31 us (11%)
  between operations  1.33 us (2%)
    pallas_call x1, Pallas kernels, local(): pl.pallas_call(functools.partial(kernel, groups, doms), out_shape=[jax.Sh...  51.7 us
    unnamed x22, local copies, waits for them, and re-layouts  6.31 us

profile of v1, /device:TPU:0, one launch (start us, length us, event | category | flops | bytes accessed | tf_op | source)
XLA Modules:
  0.0 59.3 jit_solution(992679333011733122)
XLA Ops:
  1.3 0.0 copy-start.8
  1.3 0.0 copy-start.9
  1.3 0.0 copy-start.5
  1.3 0.0 copy-start.6
  1.3 0.0 copy-start.7
  1.3 0.6 %copy-done.8 = s32[1,64]{1,0:T(1,128)S(1)} copy-done((s32[1,64]{1,0:T(1,128)S(1)}, s32[1,64]{1,0:T(1,128)}, u32[]{:S(2)}) %copy-start.8) | copy-done | bytes 280
  1.9 0.0 copy-done.9
  2.0 0.0 copy-done.5
  2.0 0.0 copy-done.6
  2.0 0.0 copy-done.7
  2.0 0.0 copy-start
  2.0 0.9 %copy-done = s32[1,4,8192]{2,1,0:T(4,128)S(1)} copy-done((s32[1,4,8192]{2,1,0:T(4,128)S(1)}, s32[1,4,8192]{2,1,0:T(4,128)}, u32[]{:S(2)}) %copy-start) | copy-done | bytes 131096
  2.9 0.0 copy-start.1
  2.9 0.9 %copy-done.1 = f32[1,3,8192]{2,0,1:T(1,128)S(1)} copy-done((f32[1,3,8192]{2,0,1:T(1,128)S(1)}, f32[1,3,8192]{2,0,1:T(1,128)}, u32[]{:S(2)}) %copy-start.1) | copy-done | bytes 98328
  3.8 0.0 copy-start.2
  3.8 0.9 %copy-done.2 = f32[1,3,8192]{2,0,1:T(1,128)S(1)} copy-done((f32[1,3,8192]{2,0,1:T(1,128)S(1)}, f32[1,3,8192]{2,0,1:T(1,128)}, u32[]{:S(2)}) %copy-start.2) | copy-done | bytes 98328
  4.7 0.0 copy-start.3
  4.7 0.9 %copy-done.3 = f32[1,3,8192]{2,0,1:T(1,128)S(1)} copy-done((f32[1,3,8192]{2,0,1:T(1,128)S(1)}, f32[1,3,8192]{2,0,1:T(1,128)}, u32[]{:S(2)}) %copy-start.3) | copy-done | bytes 98328
  5.6 0.0 copy-start.4
  5.6 0.8 %copy-done.4 = f32[1,8192]{1,0:T(1,128)S(1)} copy-done((f32[1,8192]{1,0:T(1,128)S(1)}, f32[1,8192]{1,0:T(1,128)}, u32[]{:S(2)}) %copy-start.4) | copy-done | bytes 32792
  6.4 51.7 %shell_step.1 = (f32[3,64,128]{2,1,0:T(8,128)S(1)}, f32[3,64,128]{2,1,0:T(8,128)S(1)}) custom-call(f32[3,64,128]{2,1,0:T(8,128)S(1)} %bitcast.10, f32[3,64,128]{2,1,0:T(8,128)S(1)} %bitcast.11, f32[64,128]{1,0:T(8,128)S(1)} %bitcast.15, f32[3,64,128]{2,1,0:T(8,128)S(1)} %bitcast.12, s32[4,8192]{1,0:T(4,128)S(1)} %bitcast.9, s32[4,64]{1,0:T(4,128)S(1)} %bitcast.16, ...), custom_call_target="tpu_custom_call" | custom-call | tf_op jit(solution)/shard_map/shell_step/pallas_call | solution.py:410
  58.0 0.6 %copy.20 = f32[1,3,8192]{2,0,1:T(1,128)} copy(f32[1,3,8192]{2,0,1:T(1,128)S(1)} %bitcast.14) | data formatting | bytes 196608
  58.7 0.6 %copy.21 = f32[1,3,8192]{2,0,1:T(1,128)} copy(f32[1,3,8192]{2,0,1:T(1,128)S(1)} %bitcast.13) | data formatting | bytes 196608
Async XLA Ops:
  1.3 0.7 %copy-start.8 = (s32[1,64]{1,0:T(1,128)S(1)}, s32[1,64]{1,0:T(1,128)}, u32[]{:S(2)}) copy-start(s32[1,64]{1,0:T(1,128)} %spot_ref.1) | copy-start | bytes 772
  1.3 0.7 %copy-start.9 = (s32[1,24]{1,0:T(1,128)S(1)}, s32[1,24]{1,0:T(1,128)}, u32[]{:S(2)}) copy-start(s32[1,24]{1,0:T(1,128)} %active_smem.1) | copy-start | bytes 292
  1.3 0.7 %copy-start.5 = (s32[1,4,64]{2,1,0:T(4,128)S(1)}, s32[1,4,64]{2,1,0:T(4,128)}, u32[]{:S(2)}) copy-start(s32[1,4,64]{2,1,0:T(4,128)} %param.15) | copy-start | bytes 3076
  1.3 0.7 %copy-start.6 = (s32[1,2,24]{2,1,0:T(2,128)S(1)}, s32[1,2,24]{2,1,0:T(2,128)}, u32[]{:S(2)}) copy-start(s32[1,2,24]{2,1,0:T(2,128)} %param.20) | copy-start | bytes 580
  1.3 0.7 %copy-start.7 = (s32[1,64]{1,0:T(1,128)S(1)}, s32[1,64]{1,0:T(1,128)}, u32[]{:S(2)}) copy-start(s32[1,64]{1,0:T(1,128)} %owner_ref.1) | copy-start | bytes 772
  2.0 0.9 %copy-start = (s32[1,4,8192]{2,1,0:T(4,128)S(1)}, s32[1,4,8192]{2,1,0:T(4,128)}, u32[]{:S(2)}) copy-start(s32[1,4,8192]{2,1,0:T(4,128)} %param.16) | copy-start | bytes 393220
  2.9 0.9 %copy-start.1 = (f32[1,3,8192]{2,0,1:T(1,128)S(1)}, f32[1,3,8192]{2,0,1:T(1,128)}, u32[]{:S(2)}) copy-start(f32[1,3,8192]{2,0,1:T(1,128)} %param.11) | copy-start | bytes 294916
  3.8 0.9 %copy-start.2 = (f32[1,3,8192]{2,0,1:T(1,128)S(1)}, f32[1,3,8192]{2,0,1:T(1,128)}, u32[]{:S(2)}) copy-start(f32[1,3,8192]{2,0,1:T(1,128)} %param.12) | copy-start | bytes 294916
  4.7 0.9 %copy-start.3 = (f32[1,3,8192]{2,0,1:T(1,128)S(1)}, f32[1,3,8192]{2,0,1:T(1,128)}, u32[]{:S(2)}) copy-start(f32[1,3,8192]{2,0,1:T(1,128)} %param.14) | copy-start | bytes 294916
  5.6 0.8 %copy-start.4 = (f32[1,8192]{1,0:T(1,128)S(1)}, f32[1,8192]{1,0:T(1,128)}, u32[]{:S(2)}) copy-start(f32[1,8192]{1,0:T(1,128)} %param.13) | copy-start | bytes 98308

commit v2 on v1

--- a/solution.py
+++ b/solution.py
@@ -17,6 +17,7 @@
 REACH = 1.0
 MESH = pl.DeviceIdType.MESH
 HIGHEST = lax.Precision.HIGHEST
+CHUNKS = 2
 
 
 def inner_rows(a, b):
@@ -37,6 +38,10 @@
 
 def scaled(a, s):
     return tuple(x * s for x in a)
+
+
+def gather_lanes(value, index):
+    return jnp.take_along_axis(value, index, axis=1, mode="promise_in_bounds")
 
 
 def shell_forces(pos, vel, stress_old):
@@ -113,7 +118,6 @@
     tile_out,
     inverse,
     corner_buf,
-    force_buf,
     spread,
     push_out,
     push_in,
@@ -188,35 +192,37 @@
         forward.append(copy)
     in_buf[1, g] = out_buf[g, 1]
 
-    lane16 = lax.broadcasted_iota(jnp.int32, (16, 2 * LANES), 1)
-    row16 = lax.broadcasted_iota(jnp.int32, (16, 2 * LANES), 0)
-    half = lax.div(lane16, LANES)
-    weights = jnp.where(lax.rem(lax.div(row16, 4), 2) == half, lax.rem(lane16, LANES), 0)
-    weights = weights.astype(jnp.float32).astype(jnp.bfloat16)
-    rows_of = lax.broadcasted_iota(jnp.int32, (16, LANES), 0)
-    one = jnp.ones((16, LANES), jnp.bfloat16)
-    zero = jnp.zeros((16, LANES), jnp.bfloat16)
-
-    def invert(k, carry):
-        ids = slot_ref[:, pl.ds(pl.multiple_of(k * LANES, LANES), LANES)].astype(jnp.float32)
-        level = [
-            (rows_of + 16 * j).astype(jnp.float32).astype(jnp.bfloat16) for j in range(ROWS)
-        ]
-        marks = []
-        for c in range(4):
-            here = jnp.broadcast_to(ids[c : c + 1, :], (16, LANES)).astype(jnp.bfloat16)
-            marks.append(
-                jnp.concatenate([jnp.where(here == lv, one, zero) for lv in level], 0)
-            )
-        for side, (first, second) in enumerate(((0, 3), (1, 2))):
-            both = jnp.concatenate([marks[first], marks[second]], 1)
-            found = lax.dot_general(
-                weights, both, (((1,), (1,)), ((), ())), preferred_element_type=jnp.float32
-            )
-            inverse[side, k] = found[0:ROWS, :].astype(jnp.int32)
+    sub_iota = lax.broadcasted_iota(jnp.int32, (ROWS, LANES), 0)
+    lane_iota = lax.broadcasted_iota(jnp.int32, (ROWS, LANES), 1)
+    together = blocks // ROWS // CHUNKS
+
+    def invert(chunk, carry):
+        keys = []
+        for part in range(together):
+            for c in range(4):
+                row = (chunk * together + part) * ROWS * 4 + c
+                ids = slot_ref[pl.ds(row, ROWS, stride=4), :]
+                keys.append((ids * LANES + lane_iota).astype(jnp.float32))
+        size = 2
+        while size <= LANES:
+            gap = size // 2
+            while gap >= 1:
+                other = lane_iota ^ gap
+                low = ((lane_iota & gap) == 0) == ((lane_iota & size) == 0)
+                swapped = [gather_lanes(key, other) for key in keys]
+                keys = [
+                    jnp.where(low, jnp.minimum(key, swap), jnp.maximum(key, swap))
+                    for key, swap in zip(keys, swapped)
+                ]
+                gap //= 2
+            size *= 2
+        for part in range(together):
+            here = pl.ds(pl.multiple_of((chunk * together + part) * ROWS, ROWS), ROWS)
+            for c in range(4):
+                inverse[c, here, :] = keys[part * 4 + c].astype(jnp.int32) - lane_iota * LANES
         return carry
 
-    lax.fori_loop(0, blocks, invert, 0, unroll=2)
+    lax.fori_loop(0, CHUNKS, invert, 0)
 
     for copy in forward:
         copy.wait_recv()
@@ -226,8 +232,8 @@
             canon_rows[pl.ds(layer * ROWS * ROWS + c, ROWS, stride=ROWS), :] = (
                 in_buf[0, layer, c] + in_buf[1, layer, c] + in_buf[2, layer, c]
             )
-    sub_iota = lax.broadcasted_iota(jnp.int32, (ROWS, LANES), 0)
-    lane_iota = lax.broadcasted_iota(jnp.int32, (ROWS, LANES), 1)
+    ahead = (lane_iota + sub_iota) & (LANES - 1)
+    back = (lane_iota - sub_iota) & (LANES - 1)
 
     def one_tile(t, carry):
         i = pair_smem[0, t]
@@ -236,28 +242,30 @@
         near_block = canon[i]
         far_block = canon[j]
         near = [jnp.broadcast_to(near_block[c : c + 1, :], (ROWS, LANES)) for c in range(3)]
-        far = [jnp.broadcast_to(far_block[c : c + 1, :], (ROWS, LANES)) for c in range(3)]
-        near_sum = [jnp.zeros((ROWS, LANES), jnp.float32) for _ in range(3)]
-        far_sum = [jnp.zeros((ROWS, LANES), jnp.float32) for _ in range(3)]
+        far = [
+            gather_lanes(jnp.broadcast_to(far_block[c : c + 1, :], (ROWS, LANES)), ahead)
+            for c in range(3)
+        ]
+        near_sum = [None] * 3
+        far_sum = [None] * 3
         for r in range(LANES // ROWS):
-            at = sub_iota + ROWS * r
-            diff = [
-                jnp.take_along_axis(near[c], at, axis=1, mode="promise_in_bounds") - far[c]
-                for c in range(3)
-            ]
-            weight = gain * jnp.maximum(REACH - inner_rows(diff, diff), 0.0)
+            turn = ROWS * r
+            if r:
+                turned = [pltpu.roll(far[c], LANES - turn, 1) for c in range(3)]
+            else:
+                turned = far
+            diff = [near[c] - turned[c] for c in range(3)]
+            weight = jnp.maximum(REACH - inner_rows(diff, diff), 0.0)
             for c in range(3):
                 push = weight * diff[c]
-                far_sum[c] = far_sum[c] + push
-                total = jnp.sum(push, 1, keepdims=True)
-                near_sum[c] = jnp.where(lane_iota == at, total, near_sum[c])
+                home = pltpu.roll(push, turn, 1) if r else push
+                near_sum[c] = near_sum[c] + push if r else push
+                far_sum[c] = far_sum[c] + home if r else home
         for c in range(3):
-            tile_out[c, pl.ds(t, 1), :] = jnp.sum(
-                jnp.where(lax.rem(lane_iota, ROWS) == sub_iota, near_sum[c], 0.0),
-                0,
-                keepdims=True,
+            tile_out[c, pl.ds(t, 1), :] = gain * jnp.sum(near_sum[c], 0, keepdims=True)
+            tile_out[c, pl.ds(tiles + t, 1), :] = gain * jnp.sum(
+                gather_lanes(far_sum[c], back), 0, keepdims=True
             )
-            tile_out[c, pl.ds(tiles + t, 1), :] = jnp.sum(far_sum[c], 0, keepdims=True)
         return carry
 
     lax.fori_loop(0, tiles, one_tile, 0)
@@ -292,39 +300,27 @@
     state[blocks] = ghost_in[...]
 
     def elements(part, carry):
-        for kk in range(ROWS):
-            k = part * ROWS + kk
-            at = pl.ds(pl.multiple_of(k * LANES, LANES), LANES)
-            ids = slot_ref[:, at]
-            for side, pair in enumerate(((0, 3), (1, 2))):
-                b = cb_smem[side, k]
-                block = state[b]
-                for c in pair:
-                    index = jnp.broadcast_to(ids[c : c + 1, :], (ROWS, LANES))
-                    corner_buf[c, pl.ds(kk * ROWS, ROWS), :] = jnp.take_along_axis(
-                        block, index, axis=1, mode="promise_in_bounds"
-                    )
-        pos = [[corner_buf[c, pl.ds(x, ROWS, stride=ROWS), :] for x in range(3)] for c in range(4)]
-        vel = [
-            [corner_buf[c, pl.ds(3 + x, ROWS, stride=ROWS), :] for x in range(3)] for c in range(4)
-        ]
         here = pl.ds(pl.multiple_of(part * ROWS, ROWS), ROWS)
+        for side in range(2):
+            for kk in range(ROWS):
+                b = cb_smem[side, part * ROWS + kk]
+                corner_buf[side, pl.ds(kk * ROWS, ROWS), :] = state[b]
+        pos = [None] * 4
+        vel = [None] * 4
+        for side, pair in enumerate(((0, 3), (1, 2))):
+            column = [corner_buf[side, pl.ds(x, ROWS, stride=ROWS), :] for x in range(6)]
+            for c in pair:
+                ids = slot_ref[pl.ds(part * ROWS * 4 + c, ROWS, stride=4), :]
+                picked = [gather_lanes(value, ids) for value in column]
+                pos[c] = picked[:3]
+                vel[c] = picked[3:]
         old = [stress_ref[x, here, :] for x in range(3)]
         forces, new = shell_forces(pos, vel, old)
         for x in range(3):
             stress_out[x, here, :] = new[x]
-            force_buf[0, pl.ds(x, ROWS, stride=ROWS), :] = forces[0][x]
-            force_buf[0, pl.ds(4 + x, ROWS, stride=ROWS), :] = forces[3][x]
-            force_buf[1, pl.ds(x, ROWS, stride=ROWS), :] = forces[1][x]
-            force_buf[1, pl.ds(4 + x, ROWS, stride=ROWS), :] = forces[2][x]
-        for kk in range(ROWS):
-            k = part * ROWS + kk
-            for side in range(2):
-                spread[side, pl.ds(pl.multiple_of(k * ROWS, ROWS), ROWS), :] = jnp.take_along_axis(
-                    force_buf[side, pl.ds(kk * ROWS, ROWS), :],
-                    inverse[side, k],
-                    axis=1,
-                    mode="promise_in_bounds",
+            for side, pair in enumerate(((0, 3), (1, 2))):
+                spread[side, x, here, :] = sum(
+                    gather_lanes(forces[c][x], inverse[c, here, :]) for c in pair
                 )
         return carry
 
@@ -336,12 +332,8 @@
     for c in range(3):
         total = None
         for side in range(2):
-            part = (
-                spread[side, pl.ds(c, blocks, stride=ROWS), :]
-                + spread[side, pl.ds(4 + c, blocks, stride=ROWS), :]
-            )
             value = jnp.dot(
-                hits[side], part, precision=HIGHEST, preferred_element_type=jnp.float32
+                hits[side], spread[side, c], precision=HIGHEST, preferred_element_type=jnp.float32
             )
             total = value if total is None else total + value
         internal.append(total)
@@ -422,10 +414,9 @@
             pltpu.VMEM((groups, 3, 3, ROWS, LANES), f32),
             pltpu.VMEM((slots, ROWS, LANES), f32),
             pltpu.VMEM((3, 2 * tiles, LANES), f32),
-            pltpu.VMEM((2, blocks, ROWS, LANES), jnp.int32),
-            pltpu.VMEM((4, ROWS * ROWS, LANES), f32),
+            pltpu.VMEM((4, blocks, LANES), jnp.int32),
             pltpu.VMEM((2, ROWS * ROWS, LANES), f32),
-            pltpu.VMEM((2, blocks * ROWS, LANES), f32),
+            pltpu.VMEM((2, 3, blocks, LANES), f32),
             pltpu.VMEM((ROWS, LANES), f32),
             pltpu.VMEM((ROWS, LANES), f32),
             pltpu.SemaphoreType.DMA((groups, 3)),
@@ -444,7 +435,7 @@
         velocity.reshape(3, blocks, LANES),
         mass.reshape(blocks, LANES),
         stress.reshape(3, blocks, LANES),
-        corner_slot.reshape(4, nodes),
+        corner_slot.reshape(4, blocks, LANES).transpose(1, 0, 2).reshape(4 * blocks, LANES),
         corner_block.reshape(4, blocks),
         contact_owner,
         contact_slot,

time: 59.6 us -> 37.5 us (0.63)
  Pallas kernels: 51.7 us -> 29.5 us
    pallas_call x1, Pallas kernels: 51.7 us -> 29.5 us  [local(): pl.pallas_call(functools.partial(kernel, groups, doms), out_shape=[jax.Sh...]
where the time goes in v2:
time: 37.5 us; the launch traced here: 37.1 us
  Pallas kernels  29.5 us (79%)
  local copies, waits for them, and re-layouts  6.31 us (17%)
  between operations  1.33 us (4%)
    pallas_call x1, Pallas kernels, local(): pl.pallas_call(functools.partial(kernel, groups, doms), out_shape=[jax.Sh...  29.5 us
    unnamed x22, local copies, waits for them, and re-layouts  6.31 us

profile of v2, /device:TPU:0, one launch (start us, length us, event | category | flops | bytes accessed | tf_op | source)
XLA Modules:
  0.0 37.1 jit_solution(13826135909130732515)
XLA Ops:
  1.3 0.0 copy-start.8
  1.3 0.0 copy-start.9
  1.3 0.0 copy-start.5
  1.3 0.0 copy-start.6
  1.3 0.0 copy-start.7
  1.3 0.6 %copy-done.8 = s32[1,64]{1,0:T(1,128)S(1)} copy-done((s32[1,64]{1,0:T(1,128)S(1)}, s32[1,64]{1,0:T(1,128)}, u32[]{:S(2)}) %copy-start.8) | copy-done | bytes 280
  1.9 0.0 copy-done.9
  2.0 0.0 copy-done.5
  2.0 0.0 copy-done.6
  2.0 0.0 copy-done.7
  2.0 0.0 copy-start
  2.0 0.9 %copy-done = s32[1,4,8192]{2,1,0:T(4,128)S(1)} copy-done((s32[1,4,8192]{2,1,0:T(4,128)S(1)}, s32[1,4,8192]{2,1,0:T(4,128)}, u32[]{:S(2)}) %copy-start) | copy-done | bytes 131096
  2.9 0.0 copy-start.1
  2.9 0.9 %copy-done.1 = f32[1,3,8192]{2,0,1:T(1,128)S(1)} copy-done((f32[1,3,8192]{2,0,1:T(1,128)S(1)}, f32[1,3,8192]{2,0,1:T(1,128)}, u32[]{:S(2)}) %copy-start.1) | copy-done | bytes 98328
  3.8 0.0 copy-start.2
  3.8 0.9 %copy-done.2 = f32[1,3,8192]{2,0,1:T(1,128)S(1)} copy-done((f32[1,3,8192]{2,0,1:T(1,128)S(1)}, f32[1,3,8192]{2,0,1:T(1,128)}, u32[]{:S(2)}) %copy-start.2) | copy-done | bytes 98328
  4.7 0.0 copy-start.3
  4.7 0.9 %copy-done.3 = f32[1,3,8192]{2,0,1:T(1,128)S(1)} copy-done((f32[1,3,8192]{2,0,1:T(1,128)S(1)}, f32[1,3,8192]{2,0,1:T(1,128)}, u32[]{:S(2)}) %copy-start.3) | copy-done | bytes 98328
  5.6 0.0 copy-start.4
  5.6 0.8 %copy-done.4 = f32[1,8192]{1,0:T(1,128)S(1)} copy-done((f32[1,8192]{1,0:T(1,128)S(1)}, f32[1,8192]{1,0:T(1,128)}, u32[]{:S(2)}) %copy-start.4) | copy-done | bytes 32792
  6.4 29.5 %shell_step.1 = (f32[3,64,128]{2,1,0:T(8,128)S(1)}, f32[3,64,128]{2,1,0:T(8,128)S(1)}) custom-call(f32[3,64,128]{2,1,0:T(8,128)S(1)} %bitcast.14, f32[3,64,128]{2,1,0:T(8,128)S(1)} %bitcast.15, f32[64,128]{1,0:T(8,128)S(1)} %bitcast.19, f32[3,64,128]{2,1,0:T(8,128)S(1)} %bitcast.16, s32[256,128]{1,0:T(8,128)S(1)} %bitcast.13, s32[4,64]{1,0:T(4,128)S(1)} %bitcast.20, ...), custom_call_target="tpu_custom_call" | custom-call | tf_op jit(solution)/shard_map/shell_step/pallas_call | solution.py:402
  35.8 0.6 %copy.22 = f32[1,3,8192]{2,0,1:T(1,128)} copy(f32[1,3,8192]{2,0,1:T(1,128)S(1)} %bitcast.18) | data formatting | bytes 196608
  36.5 0.6 %copy.23 = f32[1,3,8192]{2,0,1:T(1,128)} copy(f32[1,3,8192]{2,0,1:T(1,128)S(1)} %bitcast.17) | data formatting | bytes 196608
Async XLA Ops:
  1.3 0.7 %copy-start.8 = (s32[1,64]{1,0:T(1,128)S(1)}, s32[1,64]{1,0:T(1,128)}, u32[]{:S(2)}) copy-start(s32[1,64]{1,0:T(1,128)} %spot_ref.1) | copy-start | bytes 772
  1.3 0.7 %copy-start.9 = (s32[1,24]{1,0:T(1,128)S(1)}, s32[1,24]{1,0:T(1,128)}, u32[]{:S(2)}) copy-start(s32[1,24]{1,0:T(1,128)} %active_smem.1) | copy-start | bytes 292
  1.3 0.7 %copy-start.5 = (s32[1,4,64]{2,1,0:T(4,128)S(1)}, s32[1,4,64]{2,1,0:T(4,128)}, u32[]{:S(2)}) copy-start(s32[1,4,64]{2,1,0:T(4,128)} %param.15) | copy-start | bytes 3076
  1.3 0.7 %copy-start.6 = (s32[1,2,24]{2,1,0:T(2,128)S(1)}, s32[1,2,24]{2,1,0:T(2,128)}, u32[]{:S(2)}) copy-start(s32[1,2,24]{2,1,0:T(2,128)} %param.20) | copy-start | bytes 580
  1.3 0.7 %copy-start.7 = (s32[1,64]{1,0:T(1,128)S(1)}, s32[1,64]{1,0:T(1,128)}, u32[]{:S(2)}) copy-start(s32[1,64]{1,0:T(1,128)} %owner_ref.1) | copy-start | bytes 772
  2.0 0.9 %copy-start = (s32[1,4,8192]{2,1,0:T(4,128)S(1)}, s32[1,4,8192]{2,1,0:T(4,128)}, u32[]{:S(2)}) copy-start(s32[1,4,8192]{2,1,0:T(4,128)} %param.16) | copy-start | bytes 393220
  2.9 0.9 %copy-start.1 = (f32[1,3,8192]{2,0,1:T(1,128)S(1)}, f32[1,3,8192]{2,0,1:T(1,128)}, u32[]{:S(2)}) copy-start(f32[1,3,8192]{2,0,1:T(1,128)} %param.11) | copy-start | bytes 294916
  3.8 0.9 %copy-start.2 = (f32[1,3,8192]{2,0,1:T(1,128)S(1)}, f32[1,3,8192]{2,0,1:T(1,128)}, u32[]{:S(2)}) copy-start(f32[1,3,8192]{2,0,1:T(1,128)} %param.12) | copy-start | bytes 294916
  4.7 0.9 %copy-start.3 = (f32[1,3,8192]{2,0,1:T(1,128)S(1)}, f32[1,3,8192]{2,0,1:T(1,128)}, u32[]{:S(2)}) copy-start(f32[1,3,8192]{2,0,1:T(1,128)} %param.14) | copy-start | bytes 294916
  5.6 0.8 %copy-start.4 = (f32[1,8192]{1,0:T(1,128)S(1)}, f32[1,8192]{1,0:T(1,128)}, u32[]{:S(2)}) copy-start(f32[1,8192]{1,0:T(1,128)} %param.13) | copy-start | bytes 98308

commit v3 on v2

--- a/solution.py
+++ b/solution.py
@@ -17,7 +17,7 @@
 REACH = 1.0
 MESH = pl.DeviceIdType.MESH
 HIGHEST = lax.Precision.HIGHEST
-CHUNKS = 2
+BF16 = jnp.bfloat16
 
 
 def inner_rows(a, b):
@@ -42,6 +42,53 @@
 
 def gather_lanes(value, index):
     return jnp.take_along_axis(value, index, axis=1, mode="promise_in_bounds")
+
+
+def pieces(value, count):
+    parts = []
+    for _ in range(count - 1):
+        top = value.astype(BF16).astype(jnp.float32)
+        parts.append(top)
+        value = value - top
+    parts.append(value)
+    return jnp.concatenate(parts, 0).astype(BF16)
+
+
+def pick_rows(chosen, value, count):
+    lhs = jnp.concatenate([chosen] * count, 1).astype(BF16)
+    return jnp.dot(lhs, pieces(value, count), preferred_element_type=jnp.float32)
+
+
+def sort_rows(rows, sub):
+    rows = list(rows)
+    for k in range(1, 8):
+        up = None if k < 4 or k == 7 else (sub & (1 << (k - 4))) == 0
+        for j in range(k - 1, -1, -1):
+            if j >= 4:
+                gap = 1 << (j - 4)
+                keep = (sub & gap) == 0
+                if up is not None:
+                    keep = keep == up
+                for r in range(16):
+                    other = jnp.take_along_axis(
+                        rows[r], sub ^ gap, axis=0, mode="promise_in_bounds"
+                    )
+                    rows[r] = jnp.where(
+                        keep, jnp.minimum(rows[r], other), jnp.maximum(rows[r], other)
+                    )
+                continue
+            for r in range(16):
+                far = r | (1 << j)
+                if far == r:
+                    continue
+                low = jnp.minimum(rows[r], rows[far])
+                high = jnp.maximum(rows[r], rows[far])
+                if up is not None:
+                    low, high = jnp.where(up, low, high), jnp.where(up, high, low)
+                elif k < 4 and r & (1 << k):
+                    low, high = high, low
+                rows[r], rows[far] = low, high
+    return rows
 
 
 def shell_forces(pos, vel, stress_old):
@@ -92,6 +139,19 @@
 def kernel(
     groups,
     doms,
+    pos_hbm,
+    vel_hbm,
+    mass_hbm,
+    stress_hbm,
+    slot_hbm,
+    cb_hbm,
+    owner_hbm,
+    spot_hbm,
+    pair_hbm,
+    active_hbm,
+    halo_hbm,
+    vel_out,
+    stress_out,
     pos_ref,
     vel_ref,
     mass_ref,
@@ -101,12 +161,11 @@
     owner_ref,
     spot_ref,
     pair_ref,
+    active_ref,
     cb_smem,
+    pair_smem,
     halo_smem,
-    pair_smem,
-    active_smem,
-    vel_out,
-    stress_out,
+    in_sems,
     state,
     rim,
     ghost_in,
@@ -117,6 +176,7 @@
     canon,
     tile_out,
     inverse,
+    sort_buf,
     corner_buf,
     spread,
     push_out,
@@ -147,13 +207,30 @@
     for turn, k, step, dd in partners:
         pl.semaphore_signal(barrier, inc=1, device_id=(k, dd), device_id_type=MESH)
 
-    halo = halo_smem[0, 0]
-    state_rows = state.reshape((blocks + 1) * ROWS, LANES)
-    for c in range(3):
-        state_rows[pl.ds(c, blocks, stride=ROWS), :] = pos_ref[c]
-        state_rows[pl.ds(3 + c, blocks, stride=ROWS), :] = vel_ref[c]
-    rim[...] = state[halo]
-
+    sources = (
+        (pos_hbm, pos_ref),
+        (owner_hbm, owner_ref),
+        (spot_hbm, spot_ref),
+        (vel_hbm, vel_ref),
+        (halo_hbm, halo_smem),
+        (slot_hbm, slot_ref),
+        (pair_hbm, pair_ref),
+        (pair_hbm, pair_smem),
+        (active_hbm, active_ref),
+        (cb_hbm, cb_ref),
+        (cb_hbm, cb_smem),
+        (stress_hbm, stress_ref),
+        (mass_hbm, mass_ref),
+    )
+    loads = []
+    for n, (source, target) in enumerate(sources):
+        copy = pltpu.make_async_copy(source, target, in_sems.at[n])
+        copy.start()
+        loads.append(copy)
+    for copy in loads[:3]:
+        copy.wait()
+    sub_iota = lax.broadcasted_iota(jnp.int32, (ROWS, LANES), 0)
+    lane_iota = lax.broadcasted_iota(jnp.int32, (ROWS, LANES), 1)
     owner = owner_ref[...]
     step_of = lax.rem(lax.rem(owner, doms) - d + 1 + doms, doms)
     goal = (lax.div(owner, doms) * 3 + step_of) * ROWS + lax.rem(spot_ref[...], ROWS)
@@ -162,22 +239,14 @@
     chosen = (
         lax.broadcasted_iota(jnp.int32, (places, blocks), 0) == goal
     ).astype(jnp.float32)
+    everywhere = jnp.concatenate([pos_ref[c] for c in range(3)], 1)
+    packed = pick_rows(chosen, everywhere, 3)
     for c in range(3):
-        column = pos_ref[c]
-        packed = jnp.dot(chosen, column, precision=HIGHEST, preferred_element_type=jnp.float32)
-        out_buf[:, :, c, :, :] = packed.reshape(groups, 3, ROWS, LANES)
-
+        out_buf[:, :, c, :, :] = packed[:, c * LANES : (c + 1) * LANES].reshape(
+            groups, 3, ROWS, LANES
+        )
     pl.semaphore_wait(barrier, len(partners))
 
-    rim_copy = pltpu.make_async_remote_copy(
-        src_ref=rim,
-        dst_ref=ghost_in,
-        send_sem=rim_sems.at[0],
-        recv_sem=rim_sems.at[1],
-        device_id=(g, left),
-        device_id_type=MESH,
-    )
-    rim_copy.start()
     forward = []
     for turn, k, step, dd in partners:
         copy = pltpu.make_async_remote_copy(
@@ -192,60 +261,54 @@
         forward.append(copy)
     in_buf[1, g] = out_buf[g, 1]
 
-    sub_iota = lax.broadcasted_iota(jnp.int32, (ROWS, LANES), 0)
-    lane_iota = lax.broadcasted_iota(jnp.int32, (ROWS, LANES), 1)
-    together = blocks // ROWS // CHUNKS
-
-    def invert(chunk, carry):
-        keys = []
-        for part in range(together):
-            for c in range(4):
-                row = (chunk * together + part) * ROWS * 4 + c
-                ids = slot_ref[pl.ds(row, ROWS, stride=4), :]
-                keys.append((ids * LANES + lane_iota).astype(jnp.float32))
-        size = 2
-        while size <= LANES:
-            gap = size // 2
-            while gap >= 1:
-                other = lane_iota ^ gap
-                low = ((lane_iota & gap) == 0) == ((lane_iota & size) == 0)
-                swapped = [gather_lanes(key, other) for key in keys]
-                keys = [
-                    jnp.where(low, jnp.minimum(key, swap), jnp.maximum(key, swap))
-                    for key, swap in zip(keys, swapped)
-                ]
-                gap //= 2
-            size *= 2
-        for part in range(together):
-            here = pl.ds(pl.multiple_of((chunk * together + part) * ROWS, ROWS), ROWS)
-            for c in range(4):
-                inverse[c, here, :] = keys[part * 4 + c].astype(jnp.int32) - lane_iota * LANES
-        return carry
-
-    lax.fori_loop(0, CHUNKS, invert, 0)
+    for copy in loads[3:5]:
+        copy.wait()
+    halo = halo_smem[0, 0]
+    state_rows = state.reshape((blocks + 1) * ROWS, LANES)
+    for c in range(3):
+        state_rows[pl.ds(c, blocks, stride=ROWS), :] = pos_ref[c]
+        state_rows[pl.ds(3 + c, blocks, stride=ROWS), :] = vel_ref[c]
+    rim[...] = state[halo]
+    rim_copy = pltpu.make_async_remote_copy(
+        src_ref=rim,
+        dst_ref=ghost_in,
+        send_sem=rim_sems.at[0],
+        recv_sem=rim_sems.at[1],
+        device_id=(g, left),
+        device_id_type=MESH,
+    )
+    rim_copy.start()
+    for copy in loads[5:]:
+        copy.wait()
+    goers = jnp.transpose(jnp.concatenate([chosen, jnp.zeros((LANES - places, blocks), jnp.float32)], 0))
+
+    wide_iota = lax.broadcasted_iota(jnp.int32, (LANES, LANES), 1)
+    for half in range(4 * blocks // LANES):
+        rows = pl.ds(half * LANES, LANES)
+        keys = jnp.transpose((slot_ref[rows, :] * LANES + wide_iota).astype(jnp.float32))
+        keys = sort_rows([keys[r * ROWS : (r + 1) * ROWS, :] for r in range(16)], sub_iota)
+        for r in range(16):
+            sort_buf[half, pl.ds(r, ROWS, stride=16), :] = keys[r]
+        inverse[rows, :] = jnp.transpose(sort_buf[half]).astype(jnp.int32) - wide_iota * LANES
 
     for copy in forward:
         copy.wait_recv()
-    canon_rows = canon.reshape(slots * ROWS, LANES)
-    for c in range(3):
-        for layer in range(groups):
-            canon_rows[pl.ds(layer * ROWS * ROWS + c, ROWS, stride=ROWS), :] = (
-                in_buf[0, layer, c] + in_buf[1, layer, c] + in_buf[2, layer, c]
-            )
     ahead = (lane_iota + sub_iota) & (LANES - 1)
     back = (lane_iota - sub_iota) & (LANES - 1)
+    for layer in range(groups):
+        for c in range(3):
+            rows = in_buf[0, layer, c] + in_buf[1, layer, c] + in_buf[2, layer, c]
+            for spot in range(ROWS):
+                slot = layer * ROWS + spot
+                row = jnp.broadcast_to(rows[spot : spot + 1, :], (ROWS, LANES))
+                canon[slot, c] = row
+                canon[slot, 3 + c] = gather_lanes(row, ahead)
 
     def one_tile(t, carry):
-        i = pair_smem[0, t]
-        j = pair_smem[1, t]
-        gain = PENALTY * active_smem[0, t].astype(jnp.float32)
-        near_block = canon[i]
-        far_block = canon[j]
-        near = [jnp.broadcast_to(near_block[c : c + 1, :], (ROWS, LANES)) for c in range(3)]
-        far = [
-            gather_lanes(jnp.broadcast_to(far_block[c : c + 1, :], (ROWS, LANES)), ahead)
-            for c in range(3)
-        ]
+        near_block = canon[pair_smem[0, t]]
+        far_block = canon[pair_smem[1, t]]
+        near = [near_block[c] for c in range(3)]
+        far = [far_block[3 + c] for c in range(3)]
         near_sum = [None] * 3
         far_sum = [None] * 3
         for r in range(LANES // ROWS):
@@ -262,26 +325,37 @@
                 near_sum[c] = near_sum[c] + push if r else push
                 far_sum[c] = far_sum[c] + home if r else home
         for c in range(3):
-            tile_out[c, pl.ds(t, 1), :] = gain * jnp.sum(near_sum[c], 0, keepdims=True)
-            tile_out[c, pl.ds(tiles + t, 1), :] = gain * jnp.sum(
-                gather_lanes(far_sum[c], back), 0, keepdims=True
+            tile_out[t, c] = near_sum[c]
+            tile_out[t, 3 + c] = far_sum[c]
+        return carry
+
+    lax.fori_loop(0, tiles, one_tile, 0, unroll=2)
+    near_rows = []
+    far_rows = []
+    for t in range(tiles):
+        near_rows.append(
+            jnp.concatenate(
+                [jnp.sum(tile_out[t, c], 0, keepdims=True) for c in range(3)], 1
             )
-        return carry
-
-    lax.fori_loop(0, tiles, one_tile, 0)
+        )
+        far_rows.append(
+            jnp.concatenate(
+                [
+                    jnp.sum(gather_lanes(tile_out[t, 3 + c], back), 0, keepdims=True)
+                    for c in range(3)
+                ],
+                1,
+            )
+        )
     slot_iota = lax.broadcasted_iota(jnp.int32, (slots, tiles), 0)
-    take_near = (slot_iota == pair_ref[0:1, :]).astype(jnp.float32)
-    take_far = (slot_iota == pair_ref[1:2, :]).astype(jnp.float32)
+    gain = PENALTY * active_ref[...].astype(jnp.float32)
+    take_near = jnp.where(slot_iota == pair_ref[0:1, :], gain, 0.0)
+    take_far = jnp.where(slot_iota == pair_ref[1:2, :], -gain, 0.0)
+    total = pick_rows(
+        jnp.concatenate([take_near, take_far], 1), jnp.concatenate(near_rows + far_rows, 0), 2
+    )
     for c in range(3):
-        total = jnp.dot(
-            take_near, tile_out[c, 0:tiles, :], precision=HIGHEST, preferred_element_type=jnp.float32
-        ) - jnp.dot(
-            take_far,
-            tile_out[c, tiles : 2 * tiles, :],
-            precision=HIGHEST,
-            preferred_element_type=jnp.float32,
-        )
-        ans[:, c, :, :] = total.reshape(groups, ROWS, LANES)
+        ans[:, c, :, :] = total[:, c * LANES : (c + 1) * LANES].reshape(groups, ROWS, LANES)
     backward = []
     for turn, k, step, dd in partners:
         copy = pltpu.make_async_remote_copy(
@@ -320,24 +394,26 @@
             stress_out[x, here, :] = new[x]
             for side, pair in enumerate(((0, 3), (1, 2))):
                 spread[side, x, here, :] = sum(
-                    gather_lanes(forces[c][x], inverse[c, here, :]) for c in pair
+                    gather_lanes(forces[c][x], inverse[pl.ds(part * ROWS * 4 + c, ROWS, stride=4), :]) for c in pair
                 )
         return carry
 
     lax.fori_loop(0, blocks // ROWS, elements, 0)
 
     block_iota = lax.broadcasted_iota(jnp.int32, (blocks + ROWS, blocks), 0)
-    hits = [(block_iota == cb_ref[side : side + 1, :]).astype(jnp.float32) for side in range(2)]
-    internal = []
+    hits = jnp.concatenate(
+        [(block_iota == cb_ref[side : side + 1, :]).astype(jnp.float32) for side in range(2)], 1
+    )
+    both = jnp.concatenate(
+        [
+            jnp.concatenate([spread[side, c] for c in range(3)], 1)
+            for side in range(2)
+        ],
+        0,
+    )
+    internal = pick_rows(hits, both, 2)
     for c in range(3):
-        total = None
-        for side in range(2):
-            value = jnp.dot(
-                hits[side], spread[side, c], precision=HIGHEST, preferred_element_type=jnp.float32
-            )
-            total = value if total is None else total + value
-        internal.append(total)
-        push_out[pl.ds(c, 1), :] = total[blocks : blocks + 1, :]
+        push_out[pl.ds(c, 1), :] = internal[blocks : blocks + 1, c * LANES : (c + 1) * LANES]
     push_copy = pltpu.make_async_remote_copy(
         src_ref=push_out,
         dst_ref=push_in,
@@ -350,24 +426,18 @@
 
     for copy in backward:
         copy.wait_recv()
-    contact = []
-    for c in range(3):
-        answers = ret[:, :, c, :, :].reshape(places, LANES)
-        contact.append(
-            lax.dot_general(
-                chosen,
-                answers,
-                (((0,), (0,)), ((), ())),
-                precision=HIGHEST,
-                preferred_element_type=jnp.float32,
-            )
-        )
+    answers = jnp.concatenate(
+        [ret[:, :, c, :, :].reshape(places, LANES) for c in range(3)], 1
+    )
+    answers = jnp.concatenate([answers, jnp.zeros((LANES - places, 3 * LANES), jnp.float32)], 0)
+    contact = pick_rows(goers, answers, 2)
     push_copy.wait_recv()
     is_rim = lax.broadcasted_iota(jnp.int32, (blocks, LANES), 0) == halo
     factor = DT / mass_ref[...]
     for c in range(3):
         extra = jnp.where(is_rim, push_in[pl.ds(c, 1), :], 0.0)
-        force = contact[c] - internal[c][0:blocks, :] - extra
+        cols = slice(c * LANES, (c + 1) * LANES)
+        force = contact[:, cols] - internal[0:blocks, cols] - extra
         vel_out[c] = vel_ref[c] + factor * force
     rim_copy.wait_send()
     push_copy.wait_send()
@@ -397,14 +467,28 @@
     tiles = tile_pairs.shape[2]
     slots = groups * ROWS
     vmem = pl.BlockSpec(memory_space=pltpu.VMEM)
-    smem = pl.BlockSpec(memory_space=pltpu.SMEM)
+    i32 = jnp.int32
     f32 = jnp.float32
     out = pl.pallas_call(
         functools.partial(kernel, groups, doms),
         out_shape=[jax.ShapeDtypeStruct((3, blocks, LANES), f32)] * 2,
-        in_specs=[vmem] * 9 + [smem] * 4,
+        in_specs=[pl.BlockSpec(memory_space=pltpu.HBM)] * 11,
         out_specs=[vmem] * 2,
         scratch_shapes=[
+            pltpu.VMEM((3, blocks, LANES), f32),
+            pltpu.VMEM((3, blocks, LANES), f32),
+            pltpu.VMEM((blocks, LANES), f32),
+            pltpu.VMEM((3, blocks, LANES), f32),
+            pltpu.VMEM((4 * blocks, LANES), i32),
+            pltpu.VMEM((4, blocks), i32),
+            pltpu.VMEM((1, blocks), i32),
+            pltpu.VMEM((1, blocks), i32),
+            pltpu.VMEM((2, tiles), i32),
+            pltpu.VMEM((1, tiles), i32),
+            pltpu.SMEM((4, blocks), i32),
+            pltpu.SMEM((2, tiles), i32),
+            pltpu.SMEM((1, 1), i32),
+            pltpu.SemaphoreType.DMA((13,)),
             pltpu.VMEM((blocks + 1, ROWS, LANES), f32),
             pltpu.VMEM((ROWS, LANES), f32),
             pltpu.VMEM((ROWS, LANES), f32),
@@ -412,9 +496,10 @@
             pltpu.VMEM((3, groups, 3, ROWS, LANES), f32),
             pltpu.VMEM((groups, 3, ROWS, LANES), f32),
             pltpu.VMEM((groups, 3, 3, ROWS, LANES), f32),
-            pltpu.VMEM((slots, ROWS, LANES), f32),
-            pltpu.VMEM((3, 2 * tiles, LANES), f32),
-            pltpu.VMEM((4, blocks, LANES), jnp.int32),
+            pltpu.VMEM((slots, 6, ROWS, LANES), f32),
+            pltpu.VMEM((tiles, 6, ROWS, LANES), f32),
+            pltpu.VMEM((4 * blocks, LANES), jnp.int32),
+            pltpu.VMEM((4 * blocks // LANES, LANES, LANES), f32),
             pltpu.VMEM((2, ROWS * ROWS, LANES), f32),
             pltpu.VMEM((2, 3, blocks, LANES), f32),
             pltpu.VMEM((ROWS, LANES), f32),
@@ -427,7 +512,7 @@
             pltpu.SemaphoreType.DMA((2,)),
         ],
         compiler_params=pltpu.CompilerParams(
-            collective_id=0, has_side_effects=True, vmem_limit_bytes=32 * 1024 * 1024
+            collective_id=0, has_side_effects=True, vmem_limit_bytes=60 * 1024 * 1024
         ),
         name="shell_step",
     )(
@@ -440,10 +525,8 @@
         contact_owner,
         contact_slot,
         tile_pairs.reshape(2, tiles),
-        corner_block.reshape(4, blocks),
+        tile_active,
         halo_block,
-        tile_pairs.reshape(2, tiles),
-        tile_active,
     )
     return out[0].reshape(1, 3, nodes), out[1].reshape(1, 3, nodes)
 

time: 37.5 us -> 31.7 us (0.85)
  local copies, waits for them, and re-layouts: 6.31 us -> 2.22 us
  Pallas kernels: 29.5 us -> 28 us
    unnamed x22 -> x4, local copies, waits for them, and re-layouts: 6.31 us -> 2.22 us
    pallas_call x1, Pallas kernels: 29.5 us -> 28 us  [local(): pl.pallas_call(functools.partial(kernel, groups, doms), out_shape=[jax.Sh...]
where the time goes in v3:
time: 31.7 us; the launch traced here: 31.5 us
  Pallas kernels  28 us (88%)
  local copies, waits for them, and re-layouts  2.22 us (7%)
  between operations  1.3 us (4%)
    pallas_call x1, Pallas kernels, local(): pl.pallas_call(functools.partial(kernel, groups, doms), out_shape=[jax.Sh...  28 us
    unnamed x4, local copies, waits for them, and re-layouts  2.22 us

profile of v3, /device:TPU:0, one launch (start us, length us, event | category | flops | bytes accessed | tf_op | source)
XLA Modules:
  0.0 31.5 jit_solution(12345264470844917196)
XLA Ops:
  1.3 28.0 %shell_step.1 = (f32[3,64,128]{2,1,0:T(8,128)}, f32[3,64,128]{2,1,0:T(8,128)}) custom-call(f32[3,64,128]{2,1,0:T(8,128)} %bitcast.14, f32[3,64,128]{2,1,0:T(8,128)} %bitcast.15, f32[64,128]{1,0:T(8,128)} %bitcast.19, f32[3,64,128]{2,1,0:T(8,128)} %bitcast.16, s32[256,128]{1,0:T(8,128)} %bitcast.13, s32[4,64]{1,0:T(4,128)} %bitcast.20, s32[1,64]{1,0:T(1,128)} %owner_hbm.1, ...), custom_call_target="tpu_custom_call" | custom-call | tf_op jit(solution)/shard_map/shell_step/pallas_call | solution.py:472
  29.3 0.0 copy-start
  29.3 1.6 %copy.22 = f32[1,3,8192]{2,0,1:T(1,128)} copy(f32[1,3,8192]{2,0,1:T(1,128)} %bitcast.18) | data formatting | bytes 196608
  30.9 0.0 copy-done
  30.9 0.6 %copy.23 = f32[1,3,8192]{2,0,1:T(1,128)} copy(f32[1,3,8192]{2,0,1:T(1,128)S(1)} %bitcast.17) | data formatting | bytes 196608
Async XLA Ops:
  29.3 1.6 %copy-start = (f32[3,64,128]{2,1,0:T(8,128)S(1)}, f32[3,64,128]{2,1,0:T(8,128)}, u32[]{:S(2)}) copy-start(f32[3,64,128]{2,1,0:T(8,128)} %get-tuple-element.5) | copy-start | bytes 294916

commit v4 on v3

--- a/solution.py
+++ b/solution.py
@@ -18,6 +18,7 @@
 MESH = pl.DeviceIdType.MESH
 HIGHEST = lax.Precision.HIGHEST
 BF16 = jnp.bfloat16
+UNROLL = 2
 
 
 def inner_rows(a, b):
@@ -174,7 +175,13 @@
     ans,
     ret,
     canon,
-    tile_out,
+    near_pick,
+    cols_even,
+    cols_odd,
+    held_even,
+    held_odd,
+    near_sums,
+    far_sums,
     inverse,
     sort_buf,
     corner_buf,
@@ -196,7 +203,7 @@
     left = lax.rem(d + doms - 1, doms)
     right = lax.rem(d + 1, doms)
     partners = []
-    for turn in range(groups):
+    for turn in (2, 1, 3, 0):
         k = lax.rem(g + turn, groups)
         for step, dd in ((0, left), (1, d), (2, right)):
             if turn == 0 and step == 1:
@@ -291,69 +298,109 @@
             sort_buf[half, pl.ds(r, ROWS, stride=16), :] = keys[r]
         inverse[rows, :] = jnp.transpose(sort_buf[half]).astype(jnp.int32) - wide_iota * LANES
 
+    slot_iota = lax.broadcasted_iota(jnp.int32, (slots, tiles), 0)
+    gain = PENALTY * active_ref[...].astype(jnp.float32)
+    take_near = jnp.where(slot_iota == pair_ref[0:1, :], gain, 0.0).astype(BF16)
+    take_far = jnp.where(slot_iota == pair_ref[1:2, :], -gain, 0.0).astype(BF16)
+    tile_iota = lax.broadcasted_iota(jnp.int32, (tiles, 2 * LANES), 0)
+    column = lax.broadcasted_iota(jnp.int32, (tiles, 2 * LANES), 1)
+    same = ((column & (LANES - 1)) == tile_iota).astype(BF16)
+    take_near = jnp.dot(take_near, same, preferred_element_type=jnp.float32).astype(BF16)
+    tile_iota = lax.broadcasted_iota(jnp.int32, (tiles, tiles * ROWS), 0)
+    column = lax.broadcasted_iota(jnp.int32, (tiles, tiles * ROWS), 1)
+    same = (lax.div(column, ROWS) == tile_iota).astype(BF16)
+    take_far = jnp.dot(take_far, same, preferred_element_type=jnp.float32)
+    near_sums[...] = jnp.zeros_like(near_sums)
+    depth = lax.broadcasted_iota(jnp.int32, (LANES, LANES), 0)
+    depth = jnp.where(depth < 3 * slots, lax.rem(depth, slots), -1)
+
+    def pick(t, carry):
+        near_pick[t] = (depth == pair_smem[0, t]).astype(jnp.float32).astype(BF16)
+        return carry
+
+    lax.fori_loop(0, tiles, pick, 0)
+
     for copy in forward:
         copy.wait_recv()
-    ahead = (lane_iota + sub_iota) & (LANES - 1)
-    back = (lane_iota - sub_iota) & (LANES - 1)
-    for layer in range(groups):
+    cols = (cols_even, cols_odd)
+    held = (held_even, held_odd)
+    canon_rows = canon.reshape(slots * ROWS, LANES)
+    split = []
+    for c in range(3):
+        layers = []
+        for layer in range(groups):
+            rows = in_buf[0, layer, c] + in_buf[1, layer, c] + in_buf[2, layer, c]
+            canon_rows[pl.ds(layer * ROWS * ROWS + c, ROWS, stride=ROWS), :] = rows
+            layers.append(rows)
+        value = jnp.concatenate(layers, 0)
+        top = value.astype(BF16).astype(jnp.float32)
+        rest = value - top
+        middle = rest.astype(BF16).astype(jnp.float32)
+        stack = jnp.concatenate([top, middle, rest - middle, jnp.zeros_like(value)], 0)
+        split.append(jnp.transpose(stack).astype(BF16))
+    split = jnp.concatenate(split, 0)
+
+    def broadcasts(step, cols):
+        for u in range(UNROLL):
+            cols[u] = jnp.dot(
+                split, near_pick[step * UNROLL + u], preferred_element_type=jnp.float32
+            )
+
+    def lane_sums(step, held):
         for c in range(3):
-            rows = in_buf[0, layer, c] + in_buf[1, layer, c] + in_buf[2, layer, c]
-            for spot in range(ROWS):
-                slot = layer * ROWS + spot
-                row = jnp.broadcast_to(rows[spot : spot + 1, :], (ROWS, LANES))
-                canon[slot, c] = row
-                canon[slot, 3 + c] = gather_lanes(row, ahead)
-
-    def one_tile(t, carry):
-        near_block = canon[pair_smem[0, t]]
-        far_block = canon[pair_smem[1, t]]
-        near = [near_block[c] for c in range(3)]
-        far = [far_block[3 + c] for c in range(3)]
-        near_sum = [None] * 3
-        far_sum = [None] * 3
-        for r in range(LANES // ROWS):
-            turn = ROWS * r
-            if r:
-                turned = [pltpu.roll(far[c], LANES - turn, 1) for c in range(3)]
-            else:
-                turned = far
-            diff = [near[c] - turned[c] for c in range(3)]
-            weight = jnp.maximum(REACH - inner_rows(diff, diff), 0.0)
+            for r in range(LANES // ROWS):
+                rows = pl.ds(c * LANES + r * ROWS, ROWS)
+                value = near_sums[rows, :]
+                for u in range(UNROLL):
+                    total = jnp.sum(held[u, rows, :], 1, keepdims=True)
+                    value = jnp.where(lane_iota == step * UNROLL + u, total, value)
+                near_sums[rows, :] = value
+
+    def pushes(step, cols, held):
+        for u in range(UNROLL):
+            t = step * UNROLL + u
+            far_block = canon[pair_smem[1, t]]
+            far = [jnp.broadcast_to(far_block[c : c + 1, :], (ROWS, LANES)) for c in range(3)]
+            far_sum = [None] * 3
+            for r in range(LANES // ROWS):
+                rows = [pl.ds(c * LANES + r * ROWS, ROWS) for c in range(3)]
+                diff = [cols[u, rows[c], :] - far[c] for c in range(3)]
+                weight = jnp.maximum(REACH - inner_rows(diff, diff), 0.0)
+                for c in range(3):
+                    push = weight * diff[c]
+                    held[u, rows[c], :] = push
+                    far_sum[c] = far_sum[c] + push if r else push
+            place = pl.ds(pl.multiple_of(t * ROWS, ROWS), ROWS)
             for c in range(3):
-                push = weight * diff[c]
-                home = pltpu.roll(push, turn, 1) if r else push
-                near_sum[c] = near_sum[c] + push if r else push
-                far_sum[c] = far_sum[c] + home if r else home
-        for c in range(3):
-            tile_out[t, c] = near_sum[c]
-            tile_out[t, 3 + c] = far_sum[c]
+                far_sums[place, c * LANES : (c + 1) * LANES] = far_sum[c]
+
+    def tile_steps(half, carry):
+        for phase in range(2):
+            step = half * 2 + phase
+            lane_sums(step - 1, held[1 - phase])
+            pushes(step, cols[phase], held[phase])
+            broadcasts(step + 1, cols[1 - phase])
         return carry
 
-    lax.fori_loop(0, tiles, one_tile, 0, unroll=2)
-    near_rows = []
-    far_rows = []
-    for t in range(tiles):
-        near_rows.append(
-            jnp.concatenate(
-                [jnp.sum(tile_out[t, c], 0, keepdims=True) for c in range(3)], 1
+    steps = tiles // UNROLL
+    broadcasts(0, cols[0])
+    lax.fori_loop(0, steps // 2, tile_steps, 0)
+    lane_sums(steps - 1, held[1])
+    total = pick_rows(take_far, far_sums[...], 2)
+    near_total = []
+    for c in range(3):
+        value = near_sums[pl.ds(c * LANES, LANES), :]
+        top = value.astype(BF16)
+        low = (value - top.astype(jnp.float32)).astype(BF16)
+        near_total.append(
+            lax.dot_general(
+                take_near,
+                jnp.concatenate([top, low], 1),
+                (((1,), (1,)), ((), ())),
+                preferred_element_type=jnp.float32,
             )
         )
-        far_rows.append(
-            jnp.concatenate(
-                [
-                    jnp.sum(gather_lanes(tile_out[t, 3 + c], back), 0, keepdims=True)
-                    for c in range(3)
-                ],
-                1,
-            )
-        )
-    slot_iota = lax.broadcasted_iota(jnp.int32, (slots, tiles), 0)
-    gain = PENALTY * active_ref[...].astype(jnp.float32)
-    take_near = jnp.where(slot_iota == pair_ref[0:1, :], gain, 0.0)
-    take_far = jnp.where(slot_iota == pair_ref[1:2, :], -gain, 0.0)
-    total = pick_rows(
-        jnp.concatenate([take_near, take_far], 1), jnp.concatenate(near_rows + far_rows, 0), 2
-    )
+    total = total + jnp.concatenate(near_total, 1)
     for c in range(3):
         ans[:, c, :, :] = total[:, c * LANES : (c + 1) * LANES].reshape(groups, ROWS, LANES)
     backward = []
@@ -496,8 +543,14 @@
             pltpu.VMEM((3, groups, 3, ROWS, LANES), f32),
             pltpu.VMEM((groups, 3, ROWS, LANES), f32),
             pltpu.VMEM((groups, 3, 3, ROWS, LANES), f32),
-            pltpu.VMEM((slots, 6, ROWS, LANES), f32),
-            pltpu.VMEM((tiles, 6, ROWS, LANES), f32),
+            pltpu.VMEM((slots, ROWS, LANES), f32),
+            pltpu.VMEM((tiles + UNROLL, LANES, LANES), jnp.bfloat16),
+            pltpu.VMEM((UNROLL, 3 * LANES, LANES), f32),
+            pltpu.VMEM((UNROLL, 3 * LANES, LANES), f32),
+            pltpu.VMEM((UNROLL, 3 * LANES, LANES), f32),
+            pltpu.VMEM((UNROLL, 3 * LANES, LANES), f32),
+            pltpu.VMEM((3 * LANES, LANES), f32),
+            pltpu.VMEM((tiles * ROWS, 3 * LANES), f32),
             pltpu.VMEM((4 * blocks, LANES), jnp.int32),
             pltpu.VMEM((4 * blocks // LANES, LANES, LANES), f32),
             pltpu.VMEM((2, ROWS * ROWS, LANES), f32),

time: 31.7 us -> 26.9 us (0.85)
  Pallas kernels: 28 us -> 23.2 us
    pallas_call x1, Pallas kernels: 28 us -> 23.2 us  [local(): pl.pallas_call(functools.partial(kernel, groups, doms), out_shape=[jax.Sh...]
where the time goes in v4:
time: 26.9 us; the launch traced here: 26.7 us
  Pallas kernels  23.2 us (86%)
  local copies, waits for them, and re-layouts  2.22 us (8%)
  between operations  1.3 us (5%)
    pallas_call x1, Pallas kernels, local(): pl.pallas_call(functools.partial(kernel, groups, doms), out_shape=[jax.Sh...  23.2 us
    unnamed x4, local copies, waits for them, and re-layouts  2.22 us

profile of v4, /device:TPU:0, one launch (start us, length us, event | category | flops | bytes accessed | tf_op | source)
XLA Modules:
  0.0 26.7 jit_solution(18026278011558877054)
XLA Ops:
  1.3 23.2 %shell_step.1 = (f32[3,64,128]{2,1,0:T(8,128)}, f32[3,64,128]{2,1,0:T(8,128)}) custom-call(f32[3,64,128]{2,1,0:T(8,128)} %bitcast.14, f32[3,64,128]{2,1,0:T(8,128)} %bitcast.15, f32[64,128]{1,0:T(8,128)} %bitcast.19, f32[3,64,128]{2,1,0:T(8,128)} %bitcast.16, s32[256,128]{1,0:T(8,128)} %bitcast.13, s32[4,64]{1,0:T(4,128)} %bitcast.20, s32[1,64]{1,0:T(1,128)} %owner_hbm.1, ...), custom_call_target="tpu_custom_call" | custom-call | tf_op jit(solution)/shard_map/shell_step/pallas_call | solution.py:519
  24.5 0.0 copy-start
  24.5 1.6 %copy.22 = f32[1,3,8192]{2,0,1:T(1,128)} copy(f32[1,3,8192]{2,0,1:T(1,128)} %bitcast.18) | data formatting | bytes 196608
  26.1 0.0 copy-done
  26.1 0.6 %copy.23 = f32[1,3,8192]{2,0,1:T(1,128)} copy(f32[1,3,8192]{2,0,1:T(1,128)S(1)} %bitcast.17) | data formatting | bytes 196608
Async XLA Ops:
  24.5 1.6 %copy-start = (f32[3,64,128]{2,1,0:T(8,128)S(1)}, f32[3,64,128]{2,1,0:T(8,128)}, u32[]{:S(2)}) copy-start(f32[3,64,128]{2,1,0:T(8,128)} %get-tuple-element.5) | copy-start | bytes 294916

commit v5 on v4

--- a/solution.py
+++ b/solution.py
@@ -565,20 +565,20 @@
             pltpu.SemaphoreType.DMA((2,)),
         ],
         compiler_params=pltpu.CompilerParams(
-            collective_id=0, has_side_effects=True, vmem_limit_bytes=60 * 1024 * 1024
+            collective_id=0, has_side_effects=True, vmem_limit_bytes=32 * 1024 * 1024
         ),
         name="shell_step",
     )(
-        positions.reshape(3, blocks, LANES),
-        velocity.reshape(3, blocks, LANES),
-        mass.reshape(blocks, LANES),
-        stress.reshape(3, blocks, LANES),
-        corner_slot.reshape(4, blocks, LANES).transpose(1, 0, 2).reshape(4 * blocks, LANES),
-        corner_block.reshape(4, blocks),
-        contact_owner,
-        contact_slot,
-        tile_pairs.reshape(2, tiles),
-        tile_active,
+        pltpu.with_memory_space_constraint(positions.reshape(3, blocks, LANES), pltpu.HBM),
+        pltpu.with_memory_space_constraint(velocity.reshape(3, blocks, LANES), pltpu.HBM),
+        pltpu.with_memory_space_constraint(mass.reshape(blocks, LANES), pltpu.HBM),
+        pltpu.with_memory_space_constraint(stress.reshape(3, blocks, LANES), pltpu.HBM),
+        pltpu.with_memory_space_constraint(corner_slot.reshape(4, blocks, LANES).transpose(1, 0, 2).reshape(4 * blocks, LANES), pltpu.HBM),
+        pltpu.with_memory_space_constraint(corner_block.reshape(4, blocks), pltpu.HBM),
+        pltpu.with_memory_space_constraint(contact_owner, pltpu.HBM),
+        pltpu.with_memory_space_constraint(contact_slot, pltpu.HBM),
+        pltpu.with_memory_space_constraint(tile_pairs.reshape(2, tiles), pltpu.HBM),
+        pltpu.with_memory_space_constraint(tile_active, pltpu.HBM),
         halo_block,
     )
     return out[0].reshape(1, 3, nodes), out[1].reshape(1, 3, nodes)

time: 26.9 us -> 25.2 us (0.937)
  local copies, waits for them, and re-layouts: 2.22 us -> 1.28 us
  Pallas kernels: 23.2 us -> 22.5 us
    unnamed x4 -> x2, local copies, waits for them, and re-layouts: 2.22 us -> 1.28 us
    pallas_call x1, Pallas kernels: 23.2 us -> 22.5 us  [local(): pl.pallas_call(functools.partial(kernel, groups, doms), out_shape=[jax.Sh...]
where the time goes in v5:
time: 25.2 us; the launch traced here: 25.1 us
  Pallas kernels  22.5 us (89%)
  between operations  1.29 us (5%)
  local copies, waits for them, and re-layouts  1.28 us (5%)
    pallas_call x1, Pallas kernels, local(): pl.pallas_call(functools.partial(kernel, groups, doms), out_shape=[jax.Sh...  22.5 us
    unnamed x2, local copies, waits for them, and re-layouts  1.28 us

profile of v5, /device:TPU:0, one launch (start us, length us, event | category | flops | bytes accessed | tf_op | source)
XLA Modules:
  0.0 25.1 jit_solution(9753785246469269115)
XLA Ops:
  1.3 22.5 %shell_step.1 = (f32[3,64,128]{2,1,0:T(8,128)S(1)}, f32[3,64,128]{2,1,0:T(8,128)S(1)}) custom-call(f32[3,64,128]{2,1,0:T(8,128)} %bitcast.16, f32[3,64,128]{2,1,0:T(8,128)} %bitcast.17, f32[64,128]{1,0:T(8,128)} %bitcast.19, f32[3,64,128]{2,1,0:T(8,128)} %bitcast.18, s32[256,128]{1,0:T(8,128)} %bitcast.15, s32[4,64]{1,0:T(4,128)} %bitcast.20, ...), custom_call_target="tpu_custom_call" | custom-call | tf_op jit(solution)/shard_map/shell_step/pallas_call | solution.py:519
  23.8 0.6 %copy.22 = f32[1,3,8192]{2,0,1:T(1,128)} copy(f32[1,3,8192]{2,0,1:T(1,128)S(1)} %bitcast.14) | data formatting | bytes 196608
  24.5 0.6 %copy.23 = f32[1,3,8192]{2,0,1:T(1,128)} copy(f32[1,3,8192]{2,0,1:T(1,128)S(1)} %bitcast.13) | data formatting | bytes 196608

commit v6 on v5

--- a/solution.py
+++ b/solution.py
@@ -18,7 +18,7 @@
 MESH = pl.DeviceIdType.MESH
 HIGHEST = lax.Precision.HIGHEST
 BF16 = jnp.bfloat16
-UNROLL = 2
+UNROLL = 3
 
 
 def inner_rows(a, b):
@@ -164,7 +164,10 @@
     pair_ref,
     active_ref,
     cb_smem,
-    pair_smem,
+    info_smem,
+    info_out,
+    info_in,
+    info_sems,
     halo_smem,
     in_sems,
     state,
@@ -176,8 +179,6 @@
     ret,
     canon,
     near_pick,
-    cols_even,
-    cols_odd,
     held_even,
     held_odd,
     near_sums,
@@ -203,27 +204,35 @@
     left = lax.rem(d + doms - 1, doms)
     right = lax.rem(d + 1, doms)
     partners = []
-    for turn in (2, 1, 3, 0):
-        k = lax.rem(g + turn, groups)
-        for step, dd in ((0, left), (1, d), (2, right)):
-            if turn == 0 and step == 1:
+    for step in (2, 1, 0):
+        for turn in (2, 3, 1, 0):
+            if turn == 0 and step == 0:
                 continue
-            partners.append((turn, k, step, dd))
+            partners.append((turn, lax.rem(g + turn, groups), step))
 
     barrier = pltpu.get_barrier_semaphore()
-    for turn, k, step, dd in partners:
-        pl.semaphore_signal(barrier, inc=1, device_id=(k, dd), device_id_type=MESH)
+    greeted = 0
+    for ahead in (2, 1, 0, doms - 1, doms - 2):
+        for turn in (2, 3, 1, 0):
+            if turn == 0 and ahead == 0:
+                continue
+            pl.semaphore_signal(
+                barrier,
+                inc=1,
+                device_id=(lax.rem(g + turn, groups), lax.rem(d + ahead, doms)),
+                device_id_type=MESH,
+            )
+            greeted += 1
 
     sources = (
         (pos_hbm, pos_ref),
         (owner_hbm, owner_ref),
         (spot_hbm, spot_ref),
+        (pair_hbm, pair_ref),
+        (active_hbm, active_ref),
         (vel_hbm, vel_ref),
         (halo_hbm, halo_smem),
         (slot_hbm, slot_ref),
-        (pair_hbm, pair_ref),
-        (pair_hbm, pair_smem),
-        (active_hbm, active_ref),
         (cb_hbm, cb_ref),
         (cb_hbm, cb_smem),
         (stress_hbm, stress_ref),
@@ -252,23 +261,37 @@
         out_buf[:, :, c, :, :] = packed[:, c * LANES : (c + 1) * LANES].reshape(
             groups, 3, ROWS, LANES
         )
-    pl.semaphore_wait(barrier, len(partners))
+    for copy in loads[3:5]:
+        copy.wait()
+    info_out[0:2, 0:tiles] = pair_ref[...]
+    info_out[2:3, 0:tiles] = active_ref[...]
+    pl.semaphore_wait(barrier, greeted)
+
+    info_copy = pltpu.make_async_remote_copy(
+        src_ref=info_out,
+        dst_ref=info_in,
+        send_sem=info_sems.at[0],
+        recv_sem=info_sems.at[1],
+        device_id=(g, right),
+        device_id_type=MESH,
+    )
+    info_copy.start()
 
     forward = []
-    for turn, k, step, dd in partners:
+    for turn, k, step in partners:
         copy = pltpu.make_async_remote_copy(
             src_ref=out_buf.at[k, step],
             dst_ref=in_buf.at[step, g],
             send_sem=fwd_send.at[turn, step],
             recv_sem=fwd_recv.at[turn, step],
-            device_id=(k, dd),
+            device_id=(k, lax.rem(d + step, doms)),
             device_id_type=MESH,
         )
         copy.start()
         forward.append(copy)
-    in_buf[1, g] = out_buf[g, 1]
-
-    for copy in loads[3:5]:
+    in_buf[0, g] = out_buf[g, 0]
+
+    for copy in loads[5:7]:
         copy.wait()
     halo = halo_smem[0, 0]
     state_rows = state.reshape((blocks + 1) * ROWS, LANES)
@@ -285,7 +308,7 @@
         device_id_type=MESH,
     )
     rim_copy.start()
-    for copy in loads[5:]:
+    for copy in loads[7:]:
         copy.wait()
     goers = jnp.transpose(jnp.concatenate([chosen, jnp.zeros((LANES - places, blocks), jnp.float32)], 0))
 
@@ -298,10 +321,14 @@
             sort_buf[half, pl.ds(r, ROWS, stride=16), :] = keys[r]
         inverse[rows, :] = jnp.transpose(sort_buf[half]).astype(jnp.int32) - wide_iota * LANES
 
+    info_copy.wait_recv()
+    to_smem = pltpu.make_async_copy(info_in, info_smem, info_sems.at[2])
+    to_smem.start()
+    to_smem.wait()
     slot_iota = lax.broadcasted_iota(jnp.int32, (slots, tiles), 0)
-    gain = PENALTY * active_ref[...].astype(jnp.float32)
-    take_near = jnp.where(slot_iota == pair_ref[0:1, :], gain, 0.0).astype(BF16)
-    take_far = jnp.where(slot_iota == pair_ref[1:2, :], -gain, 0.0).astype(BF16)
+    gain = PENALTY * info_in[2:3, 0:tiles].astype(jnp.float32)
+    take_near = jnp.where(slot_iota == info_in[0:1, 0:tiles], gain, 0.0).astype(BF16)
+    take_far = jnp.where(slot_iota == info_in[1:2, 0:tiles], -gain, 0.0).astype(BF16)
     tile_iota = lax.broadcasted_iota(jnp.int32, (tiles, 2 * LANES), 0)
     column = lax.broadcasted_iota(jnp.int32, (tiles, 2 * LANES), 1)
     same = ((column & (LANES - 1)) == tile_iota).astype(BF16)
@@ -315,14 +342,13 @@
     depth = jnp.where(depth < 3 * slots, lax.rem(depth, slots), -1)
 
     def pick(t, carry):
-        near_pick[t] = (depth == pair_smem[0, t]).astype(jnp.float32).astype(BF16)
+        near_pick[t] = (depth == info_smem[0, t]).astype(jnp.float32).astype(BF16)
         return carry
 
     lax.fori_loop(0, tiles, pick, 0)
 
     for copy in forward:
         copy.wait_recv()
-    cols = (cols_even, cols_odd)
     held = (held_even, held_odd)
     canon_rows = canon.reshape(slots * ROWS, LANES)
     split = []
@@ -338,13 +364,9 @@
         middle = rest.astype(BF16).astype(jnp.float32)
         stack = jnp.concatenate([top, middle, rest - middle, jnp.zeros_like(value)], 0)
         split.append(jnp.transpose(stack).astype(BF16))
-    split = jnp.concatenate(split, 0)
-
-    def broadcasts(step, cols):
-        for u in range(UNROLL):
-            cols[u] = jnp.dot(
-                split, near_pick[step * UNROLL + u], preferred_element_type=jnp.float32
-            )
+    split = jnp.concatenate(
+        [split[c][16 * r : 16 * r + 16] for r in range(LANES // 16) for c in range(3)], 0
+    )
 
     def lane_sums(step, held):
         for c in range(3):
@@ -356,15 +378,17 @@
                     value = jnp.where(lane_iota == step * UNROLL + u, total, value)
                 near_sums[rows, :] = value
 
-    def pushes(step, cols, held):
+    def pushes(step, held):
         for u in range(UNROLL):
             t = step * UNROLL + u
-            far_block = canon[pair_smem[1, t]]
+            far_block = canon[info_smem[1, t]]
             far = [jnp.broadcast_to(far_block[c : c + 1, :], (ROWS, LANES)) for c in range(3)]
+            near = jnp.dot(split, near_pick[t], preferred_element_type=jnp.float32)
             far_sum = [None] * 3
             for r in range(LANES // ROWS):
                 rows = [pl.ds(c * LANES + r * ROWS, ROWS) for c in range(3)]
-                diff = [cols[u, rows[c], :] - far[c] for c in range(3)]
+                spots = [(r // 2 * 3 + c) * 16 + r % 2 * ROWS for c in range(3)]
+                diff = [near[spots[c] : spots[c] + ROWS, :] - far[c] for c in range(3)]
                 weight = jnp.maximum(REACH - inner_rows(diff, diff), 0.0)
                 for c in range(3):
                     push = weight * diff[c]
@@ -378,12 +402,10 @@
         for phase in range(2):
             step = half * 2 + phase
             lane_sums(step - 1, held[1 - phase])
-            pushes(step, cols[phase], held[phase])
-            broadcasts(step + 1, cols[1 - phase])
+            pushes(step, held[phase])
         return carry
 
     steps = tiles // UNROLL
-    broadcasts(0, cols[0])
     lax.fori_loop(0, steps // 2, tile_steps, 0)
     lane_sums(steps - 1, held[1])
     total = pick_rows(take_far, far_sums[...], 2)
@@ -404,18 +426,18 @@
     for c in range(3):
         ans[:, c, :, :] = total[:, c * LANES : (c + 1) * LANES].reshape(groups, ROWS, LANES)
     backward = []
-    for turn, k, step, dd in partners:
+    for turn, k, step in partners:
         copy = pltpu.make_async_remote_copy(
             src_ref=ans.at[k],
-            dst_ref=ret.at[g, 2 - step],
+            dst_ref=ret.at[g, step],
             send_sem=back_send.at[turn, step],
             recv_sem=back_recv.at[turn, step],
-            device_id=(k, dd),
+            device_id=(k, lax.rem(d + doms - step, doms)),
             device_id_type=MESH,
         )
         copy.start()
         backward.append(copy)
-    ret[g, 1] = ans[g]
+    ret[g, 0] = ans[g]
 
     rim_copy.wait_recv()
     state[blocks] = ghost_in[...]
@@ -487,6 +509,7 @@
         force = contact[:, cols] - internal[0:blocks, cols] - extra
         vel_out[c] = vel_ref[c] + factor * force
     rim_copy.wait_send()
+    info_copy.wait_send()
     push_copy.wait_send()
     for copy in forward:
         copy.wait_send()
@@ -533,9 +556,12 @@
             pltpu.VMEM((2, tiles), i32),
             pltpu.VMEM((1, tiles), i32),
             pltpu.SMEM((4, blocks), i32),
-            pltpu.SMEM((2, tiles), i32),
+            pltpu.SMEM((ROWS, LANES), i32),
+            pltpu.VMEM((ROWS, LANES), i32),
+            pltpu.VMEM((ROWS, LANES), i32),
+            pltpu.SemaphoreType.DMA((3,)),
             pltpu.SMEM((1, 1), i32),
-            pltpu.SemaphoreType.DMA((13,)),
+            pltpu.SemaphoreType.DMA((12,)),
             pltpu.VMEM((blocks + 1, ROWS, LANES), f32),
             pltpu.VMEM((ROWS, LANES), f32),
             pltpu.VMEM((ROWS, LANES), f32),
@@ -545,8 +571,6 @@
             pltpu.VMEM((groups, 3, 3, ROWS, LANES), f32),
             pltpu.VMEM((slots, ROWS, LANES), f32),
             pltpu.VMEM((tiles + UNROLL, LANES, LANES), jnp.bfloat16),
-            pltpu.VMEM((UNROLL, 3 * LANES, LANES), f32),
-            pltpu.VMEM((UNROLL, 3 * LANES, LANES), f32),
             pltpu.VMEM((UNROLL, 3 * LANES, LANES), f32),
             pltpu.VMEM((UNROLL, 3 * LANES, LANES), f32),
             pltpu.VMEM((3 * LANES, LANES), f32),

time: 25.2 us -> 24.1 us (0.956)
  the two profiles are of different devices: /device:TPU:0 before, /device:TPU:1 now
where the time goes in v6:
time: 24.1 us; the launch traced here: 23.9 us
  Pallas kernels  21.4 us (89%)
  between operations  1.29 us (5%)
  local copies, waits for them, and re-layouts  1.28 us (5%)
    pallas_call x1, Pallas kernels, local(): pl.pallas_call(functools.partial(kernel, groups, doms), out_shape=[jax.Sh...  21.4 us
    unnamed x2, local copies, waits for them, and re-layouts  1.28 us

profile of v6, /device:TPU:1, one launch (start us, length us, event | category | flops | bytes accessed | tf_op | source)
XLA Modules:
  0.0 23.9 jit_solution(4651760065801096079)
XLA Ops:
  1.3 21.4 %shell_step.1 = (f32[3,64,128]{2,1,0:T(8,128)S(1)}, f32[3,64,128]{2,1,0:T(8,128)S(1)}) custom-call(f32[3,64,128]{2,1,0:T(8,128)} %bitcast.16, f32[3,64,128]{2,1,0:T(8,128)} %bitcast.17, f32[64,128]{1,0:T(8,128)} %bitcast.19, f32[3,64,128]{2,1,0:T(8,128)} %bitcast.18, s32[256,128]{1,0:T(8,128)} %bitcast.15, s32[4,64]{1,0:T(4,128)} %bitcast.20, ...), custom_call_target="tpu_custom_call" | custom-call | tf_op jit(solution)/shard_map/shell_step/pallas_call | solution.py:542
  22.6 0.6 %copy.22 = f32[1,3,8192]{2,0,1:T(1,128)} copy(f32[1,3,8192]{2,0,1:T(1,128)S(1)} %bitcast.14) | data formatting | bytes 196608
  23.3 0.6 %copy.23 = f32[1,3,8192]{2,0,1:T(1,128)} copy(f32[1,3,8192]{2,0,1:T(1,128)S(1)} %bitcast.13) | data formatting | bytes 196608

commit v7 on v6

--- a/solution.py
+++ b/solution.py
@@ -168,6 +168,7 @@
     info_out,
     info_in,
     info_sems,
+    rim_ready,
     halo_smem,
     in_sems,
     state,
@@ -211,18 +212,13 @@
             partners.append((turn, lax.rem(g + turn, groups), step))
 
     barrier = pltpu.get_barrier_semaphore()
-    greeted = 0
-    for ahead in (2, 1, 0, doms - 1, doms - 2):
-        for turn in (2, 3, 1, 0):
-            if turn == 0 and ahead == 0:
-                continue
-            pl.semaphore_signal(
-                barrier,
-                inc=1,
-                device_id=(lax.rem(g + turn, groups), lax.rem(d + ahead, doms)),
-                device_id_type=MESH,
-            )
-            greeted += 1
+    for turn, k, step in partners:
+        pl.semaphore_signal(
+            barrier,
+            inc=1,
+            device_id=(k, lax.rem(d + doms - step, doms)),
+            device_id_type=MESH,
+        )
 
     sources = (
         (pos_hbm, pos_ref),
@@ -265,7 +261,8 @@
         copy.wait()
     info_out[0:2, 0:tiles] = pair_ref[...]
     info_out[2:3, 0:tiles] = active_ref[...]
-    pl.semaphore_wait(barrier, greeted)
+    pl.semaphore_wait(barrier, len(partners))
+    pl.semaphore_signal(rim_ready, inc=1, device_id=(g, right), device_id_type=MESH)
 
     info_copy = pltpu.make_async_remote_copy(
         src_ref=info_out,
@@ -299,15 +296,6 @@
         state_rows[pl.ds(c, blocks, stride=ROWS), :] = pos_ref[c]
         state_rows[pl.ds(3 + c, blocks, stride=ROWS), :] = vel_ref[c]
     rim[...] = state[halo]
-    rim_copy = pltpu.make_async_remote_copy(
-        src_ref=rim,
-        dst_ref=ghost_in,
-        send_sem=rim_sems.at[0],
-        recv_sem=rim_sems.at[1],
-        device_id=(g, left),
-        device_id_type=MESH,
-    )
-    rim_copy.start()
     for copy in loads[7:]:
         copy.wait()
     goers = jnp.transpose(jnp.concatenate([chosen, jnp.zeros((LANES - places, blocks), jnp.float32)], 0))
@@ -320,6 +308,17 @@
         for r in range(16):
             sort_buf[half, pl.ds(r, ROWS, stride=16), :] = keys[r]
         inverse[rows, :] = jnp.transpose(sort_buf[half]).astype(jnp.int32) - wide_iota * LANES
+
+    pl.semaphore_wait(rim_ready, 1)
+    rim_copy = pltpu.make_async_remote_copy(
+        src_ref=rim,
+        dst_ref=ghost_in,
+        send_sem=rim_sems.at[0],
+        recv_sem=rim_sems.at[1],
+        device_id=(g, left),
+        device_id_type=MESH,
+    )
+    rim_copy.start()
 
     info_copy.wait_recv()
     to_smem = pltpu.make_async_copy(info_in, info_smem, info_sems.at[2])
@@ -560,6 +559,7 @@
             pltpu.VMEM((ROWS, LANES), i32),
             pltpu.VMEM((ROWS, LANES), i32),
             pltpu.SemaphoreType.DMA((3,)),
+            pltpu.SemaphoreType.REGULAR,
             pltpu.SMEM((1, 1), i32),
             pltpu.SemaphoreType.DMA((12,)),
             pltpu.VMEM((blocks + 1, ROWS, LANES), f32),

time: 24.1 us -> 22.4 us (0.929)
  Pallas kernels: 21.4 us -> 19.7 us
    pallas_call x1, Pallas kernels: 21.4 us -> 19.7 us  [local(): pl.pallas_call(functools.partial(kernel, groups, doms), out_shape=[jax.Sh...]
where the time goes in v7:
time: 22.4 us; the launch traced here: 22.3 us
  Pallas kernels  19.7 us (88%)
  between operations  1.29 us (6%)
  local copies, waits for them, and re-layouts  1.28 us (6%)
    pallas_call x1, Pallas kernels, local(): pl.pallas_call(functools.partial(kernel, groups, doms), out_shape=[jax.Sh...  19.7 us
    unnamed x2, local copies, waits for them, and re-layouts  1.28 us

profile of v7, /device:TPU:1, one launch (start us, length us, event | category | flops | bytes accessed | tf_op | source)
XLA Modules:
  0.0 22.3 jit_solution(8174387592830755565)
XLA Ops:
  1.3 19.7 %shell_step.1 = (f32[3,64,128]{2,1,0:T(8,128)S(1)}, f32[3,64,128]{2,1,0:T(8,128)S(1)}) custom-call(f32[3,64,128]{2,1,0:T(8,128)} %bitcast.16, f32[3,64,128]{2,1,0:T(8,128)} %bitcast.17, f32[64,128]{1,0:T(8,128)} %bitcast.19, f32[3,64,128]{2,1,0:T(8,128)} %bitcast.18, s32[256,128]{1,0:T(8,128)} %bitcast.15, s32[4,64]{1,0:T(4,128)} %bitcast.20, ...), custom_call_target="tpu_custom_call" | custom-call | tf_op jit(solution)/shard_map/shell_step/pallas_call | solution.py:541
  21.0 0.6 %copy.22 = f32[1,3,8192]{2,0,1:T(1,128)} copy(f32[1,3,8192]{2,0,1:T(1,128)S(1)} %bitcast.14) | data formatting | bytes 196608
  21.7 0.6 %copy.23 = f32[1,3,8192]{2,0,1:T(1,128)} copy(f32[1,3,8192]{2,0,1:T(1,128)S(1)} %bitcast.13) | data formatting | bytes 196608

commit v8 on v7

--- a/solution.py
+++ b/solution.py
@@ -466,7 +466,7 @@
                 )
         return carry
 
-    lax.fori_loop(0, blocks // ROWS, elements, 0)
+    lax.fori_loop(0, blocks // ROWS, elements, 0, unroll=2)
 
     block_iota = lax.broadcasted_iota(jnp.int32, (blocks + ROWS, blocks), 0)
     hits = jnp.concatenate(

time: 22.4 us -> 22.1 us (0.987)
  the two profiles are of different devices: /device:TPU:1 before, /device:TPU:0 now
where the time goes in v8:
time: 22.1 us; the launch traced here: 21.8 us
  Pallas kernels  19.3 us (87%)
  between operations  1.29 us (6%)
  local copies, waits for them, and re-layouts  1.28 us (6%)
    pallas_call x1, Pallas kernels, local(): pl.pallas_call(functools.partial(kernel, groups, doms), out_shape=[jax.Sh...  19.3 us
    unnamed x2, local copies, waits for them, and re-layouts  1.28 us

profile of v8, /device:TPU:0, one launch (start us, length us, event | category | flops | bytes accessed | tf_op | source)
XLA Modules:
  0.0 21.8 jit_solution(13380290162786510848)
XLA Ops:
  1.3 19.3 %shell_step.1 = (f32[3,64,128]{2,1,0:T(8,128)S(1)}, f32[3,64,128]{2,1,0:T(8,128)S(1)}) custom-call(f32[3,64,128]{2,1,0:T(8,128)} %bitcast.16, f32[3,64,128]{2,1,0:T(8,128)} %bitcast.17, f32[64,128]{1,0:T(8,128)} %bitcast.19, f32[3,64,128]{2,1,0:T(8,128)} %bitcast.18, s32[256,128]{1,0:T(8,128)} %bitcast.15, s32[4,64]{1,0:T(4,128)} %bitcast.20, ...), custom_call_target="tpu_custom_call" | custom-call | tf_op jit(solution)/shard_map/shell_step/pallas_call | solution.py:541
  20.6 0.6 %copy.22 = f32[1,3,8192]{2,0,1:T(1,128)} copy(f32[1,3,8192]{2,0,1:T(1,128)S(1)} %bitcast.14) | data formatting | bytes 196608
  21.2 0.6 %copy.23 = f32[1,3,8192]{2,0,1:T(1,128)} copy(f32[1,3,8192]{2,0,1:T(1,128)S(1)} %bitcast.13) | data formatting | bytes 196608

commit v9 on v8

--- a/solution.py
+++ b/solution.py
@@ -309,6 +309,12 @@
             sort_buf[half, pl.ds(r, ROWS, stride=16), :] = keys[r]
         inverse[rows, :] = jnp.transpose(sort_buf[half]).astype(jnp.int32) - wide_iota * LANES
 
+    block_iota = lax.broadcasted_iota(jnp.int32, (blocks + 2 * ROWS, blocks), 0)
+    hits = jnp.concatenate(
+        [(block_iota == cb_ref[side : side + 1, :]).astype(jnp.float32) for side in range(2)], 1
+    )
+    hits = jnp.concatenate([hits, hits], 1).astype(BF16)
+    factor = DT / mass_ref[...]
     pl.semaphore_wait(rim_ready, 1)
     rim_copy = pltpu.make_async_remote_copy(
         src_ref=rim,
@@ -468,10 +474,6 @@
 
     lax.fori_loop(0, blocks // ROWS, elements, 0, unroll=2)
 
-    block_iota = lax.broadcasted_iota(jnp.int32, (blocks + ROWS, blocks), 0)
-    hits = jnp.concatenate(
-        [(block_iota == cb_ref[side : side + 1, :]).astype(jnp.float32) for side in range(2)], 1
-    )
     both = jnp.concatenate(
         [
             jnp.concatenate([spread[side, c] for c in range(3)], 1)
@@ -479,9 +481,12 @@
         ],
         0,
     )
-    internal = pick_rows(hits, both, 2)
-    for c in range(3):
-        push_out[pl.ds(c, 1), :] = internal[blocks : blocks + 1, c * LANES : (c + 1) * LANES]
+    both = pieces(both, 2)
+    shared = jnp.dot(
+        hits[blocks : blocks + 2 * ROWS], both, preferred_element_type=jnp.float32
+    )
+    for c in range(3):
+        push_out[pl.ds(c, 1), :] = shared[0:1, c * LANES : (c + 1) * LANES]
     push_copy = pltpu.make_async_remote_copy(
         src_ref=push_out,
         dst_ref=push_in,
@@ -491,6 +496,7 @@
         device_id_type=MESH,
     )
     push_copy.start()
+    internal = jnp.dot(hits[0:blocks], both, preferred_element_type=jnp.float32)
 
     for copy in backward:
         copy.wait_recv()
@@ -501,11 +507,10 @@
     contact = pick_rows(goers, answers, 2)
     push_copy.wait_recv()
     is_rim = lax.broadcasted_iota(jnp.int32, (blocks, LANES), 0) == halo
-    factor = DT / mass_ref[...]
     for c in range(3):
         extra = jnp.where(is_rim, push_in[pl.ds(c, 1), :], 0.0)
         cols = slice(c * LANES, (c + 1) * LANES)
-        force = contact[:, cols] - internal[0:blocks, cols] - extra
+        force = contact[:, cols] - internal[:, cols] - extra
         vel_out[c] = vel_ref[c] + factor * force
     rim_copy.wait_send()
     info_copy.wait_send()

time: 22.1 us -> 22 us (level)
  no operation moved by 1% of the time
where the time goes in v9:
time: 22 us; the launch traced here: 21.8 us
  Pallas kernels  19.2 us (87%)
  between operations  1.29 us (6%)
  local copies, waits for them, and re-layouts  1.28 us (6%)
    pallas_call x1, Pallas kernels, local(): pl.pallas_call(functools.partial(kernel, groups, doms), out_shape=[jax.Sh...  19.2 us
    unnamed x2, local copies, waits for them, and re-layouts  1.28 us

profile of v9, /device:TPU:0, one launch (start us, length us, event | category | flops | bytes accessed | tf_op | source)
XLA Modules:
  0.0 21.8 jit_solution(18158659696907982233)
XLA Ops:
  1.3 19.2 %shell_step.1 = (f32[3,64,128]{2,1,0:T(8,128)S(1)}, f32[3,64,128]{2,1,0:T(8,128)S(1)}) custom-call(f32[3,64,128]{2,1,0:T(8,128)} %bitcast.16, f32[3,64,128]{2,1,0:T(8,128)} %bitcast.17, f32[64,128]{1,0:T(8,128)} %bitcast.19, f32[3,64,128]{2,1,0:T(8,128)} %bitcast.18, s32[256,128]{1,0:T(8,128)} %bitcast.15, s32[4,64]{1,0:T(4,128)} %bitcast.20, ...), custom_call_target="tpu_custom_call" | custom-call | tf_op jit(solution)/shard_map/shell_step/pallas_call | solution.py:546
  20.5 0.6 %copy.22 = f32[1,3,8192]{2,0,1:T(1,128)} copy(f32[1,3,8192]{2,0,1:T(1,128)S(1)} %bitcast.14) | data formatting | bytes 196608
  21.1 0.6 %copy.23 = f32[1,3,8192]{2,0,1:T(1,128)} copy(f32[1,3,8192]{2,0,1:T(1,128)S(1)} %bitcast.13) | data formatting | bytes 196608

commit v10 on v9

--- a/solution.py
+++ b/solution.py
@@ -472,7 +472,7 @@
                 )
         return carry
 
-    lax.fori_loop(0, blocks // ROWS, elements, 0, unroll=2)
+    lax.fori_loop(0, blocks // ROWS, elements, 0, unroll=4)
 
     both = jnp.concatenate(
         [

time: 22 us -> 22 us (level)
  no operation moved by 1% of the time
where the time goes in v10:
time: 22 us; the launch traced here: 21.8 us
  Pallas kernels  19.2 us (87%)
  between operations  1.29 us (6%)
  local copies, waits for them, and re-layouts  1.28 us (6%)
    pallas_call x1, Pallas kernels, local(): pl.pallas_call(functools.partial(kernel, groups, doms), out_shape=[jax.Sh...  19.2 us
    unnamed x2, local copies, waits for them, and re-layouts  1.28 us

profile of v10, /device:TPU:0, one launch (start us, length us, event | category | flops | bytes accessed | tf_op | source)
XLA Modules:
  0.0 21.8 jit_solution(5365412889628783188)
XLA Ops:
  1.3 19.2 %shell_step.1 = (f32[3,64,128]{2,1,0:T(8,128)S(1)}, f32[3,64,128]{2,1,0:T(8,128)S(1)}) custom-call(f32[3,64,128]{2,1,0:T(8,128)} %bitcast.16, f32[3,64,128]{2,1,0:T(8,128)} %bitcast.17, f32[64,128]{1,0:T(8,128)} %bitcast.19, f32[3,64,128]{2,1,0:T(8,128)} %bitcast.18, s32[256,128]{1,0:T(8,128)} %bitcast.15, s32[4,64]{1,0:T(4,128)} %bitcast.20, ...), custom_call_target="tpu_custom_call" | custom-call | tf_op jit(solution)/shard_map/shell_step/pallas_call | solution.py:546
  20.5 0.6 %copy.22 = f32[1,3,8192]{2,0,1:T(1,128)} copy(f32[1,3,8192]{2,0,1:T(1,128)S(1)} %bitcast.14) | data formatting | bytes 196608
  21.1 0.6 %copy.23 = f32[1,3,8192]{2,0,1:T(1,128)} copy(f32[1,3,8192]{2,0,1:T(1,128)S(1)} %bitcast.13) | data formatting | bytes 196608
